TPU v7x, 128 devices: a whole 4x4x4 slice. The times are simulated.
128 devices in a mesh: section: 8 (over x, z_hi), dp: 16 (over y, z_lo, core).
Axes of the slice: x: 4, y: 4, z: 4 (z_hi: 2, z_lo: 2; z = z_hi * 2 + z_lo), core: 2. Of those that a mesh axis runs over, the one named last changes fastest.
Arguments:
- tokens: bfloat16 [2, 4, 896, 2048], P(None, None, 'dp'), may hold values from -6 to 6
- targets: bfloat16 [2, 4, 896, 2048], P(None, None, 'dp'), may hold values from -6 to 6
- weights: bfloat16 [8, 2, 2, 96, 128, 128], P('section'), as said below
- pattern: int32 [8, 2, 2, 96, 2], P('section'), may hold values from 0 to 63, as said below
- master: float32 [8, 2, 96, 128, 128], P('section', None, None, 'dp'), may hold values from -0.6 to 0.6
- moment: float32 [8, 2, 96, 128, 128], P('section', None, None, 'dp'), as said below
- variance: float32 [8, 2, 96, 128, 128], P('section', None, None, 'dp'), as said below
Outputs:
- adam_step: float32 [8, 2, 96, 128, 128], P('section', None, None, 'dp')
- new_master: float32 [8, 2, 96, 128, 128], P('section', None, None, 'dp')
Inputs may be any that keep to these rules, and one draw needn't show every extreme that they name: Within one layer and projection the 96 blocks are distinct and sorted; every block column of the up projection and every block row of the down projection holds one or more blocks. pattern[s,1] equals pattern[7 - s, 0]. Up blocks have rows below 16 and columns below 64, down blocks the reverse. weights[s,1] equals weights[7 - s, 0]; entries are scaled by the inverse root of the mean number of inputs per output. `moment`: of the order of the gradient. `variance`: Positive, of the order of the squared gradient.
All inputs are finite; a program needn't handle non-finite values.
Results may differ from a plain program's by a relative error of at most 0.022.
Values may be sent and summed in bfloat16 or wider, within the bound.
A program may use at most 192 MiB of HBM per device.

v0:
```python
import jax
import jax.numpy as jnp
from jax import lax
from jax.sharding import PartitionSpec as P

D = 2048
FF = 8192
BS = 128


norm_eps = 1e-06
gelu_coef = 0.7978845608028654
beta_first = 0.9
beta_second = 0.95
adam_eps = 1e-08
learn_rate = 0.001
decay_rate = 0.1
update_count = 10


def from_behind(x, axis, by):
    devices = lax.axis_size(axis)
    pairs = [(i, i + by) for i in range(devices) if 0 <= i + by < devices]
    return lax.ppermute(x, axis, pairs)


def partner(x, axis, stride):
    return lax.ppermute(x, axis, [(i, i ^ 1 << stride) for i in range(lax.axis_size(axis))])


def sparse_product(left_rows, blocks, take_index, put_index, out_blocks):
    row_count = left_rows.shape[0]
    picked = jnp.take(left_rows.reshape(row_count, -1, BS), take_index, axis=1)
    product = jnp.einsum("rka,kab->krb", picked, blocks, preferred_element_type=jnp.float32)
    summed = jax.ops.segment_sum(product, put_index, num_segments=out_blocks)
    return summed.transpose(1, 0, 2).reshape(row_count, out_blocks * BS)


def sparse_transposed(left_rows, blocks, take_index, put_index, out_blocks):
    row_count = left_rows.shape[0]
    picked = jnp.take(left_rows.reshape(row_count, -1, BS), take_index, axis=1)
    product = jnp.einsum("rkb,kab->kra", picked, blocks, preferred_element_type=jnp.float32)
    summed = jax.ops.segment_sum(product, put_index, num_segments=out_blocks)
    return summed.transpose(1, 0, 2).reshape(row_count, out_blocks * BS)


def gelu_slope(preact):
    tanh_input = gelu_coef * (preact + 0.044715 * preact**3)
    tangent = jnp.tanh(tanh_input)
    return 0.5 * (1.0 + tangent) + 0.5 * preact * (1.0 - tangent * tangent) * gelu_coef * (
        1.0 + 3.0 * 0.044715 * preact * preact
    )


def layer_forward(inputs, layer_weights, layer_pattern):
    widened = inputs.astype(jnp.float32)
    factor = lax.rsqrt(jnp.mean(widened * widened, axis=-1, keepdims=True) + norm_eps)
    normed = (widened * factor).astype(jnp.bfloat16)
    preact = sparse_product(
        normed, layer_weights[0], layer_pattern[0, :, 0], layer_pattern[0, :, 1], FF // BS
    )
    hidden = jax.nn.gelu(preact, approximate=True).astype(jnp.bfloat16)
    mixed = sparse_product(
        hidden, layer_weights[1], layer_pattern[1, :, 0], layer_pattern[1, :, 1], D // BS
    )
    result = (widened + mixed).astype(jnp.bfloat16)
    return (result, normed, preact, hidden)


def layer_backward(inputs, preact, upstream, layer_weights, layer_pattern):
    grad_hidden = sparse_transposed(
        upstream, layer_weights[1], layer_pattern[1, :, 1], layer_pattern[1, :, 0], FF // BS
    )
    grad_preact = (grad_hidden * gelu_slope(preact)).astype(jnp.bfloat16)
    grad_normed = sparse_transposed(
        grad_preact, layer_weights[0], layer_pattern[0, :, 1], layer_pattern[0, :, 0], D // BS
    )
    widened = inputs.astype(jnp.float32)
    factor = lax.rsqrt(jnp.mean(widened * widened, axis=-1, keepdims=True) + norm_eps)
    coupling = jnp.mean(widened * grad_normed, axis=-1, keepdims=True)
    downstream = (
        upstream.astype(jnp.float32) + factor * grad_normed - widened * factor**3 * coupling
    )
    return (downstream.astype(jnp.bfloat16), grad_preact)


def block_pairs(left_rows, right_rows, left_index, right_index):
    row_count = left_rows.shape[0]
    left_picked = jnp.take(left_rows.reshape(row_count, -1, BS), left_index, axis=1)
    right_picked = jnp.take(right_rows.reshape(row_count, -1, BS), right_index, axis=1)
    return jnp.einsum("rka,rkb->kab", left_picked, right_picked, preferred_element_type=jnp.float32)


def weight_grads(normed, grad_preact, hidden, upstream, layer_pattern):
    up_part = block_pairs(normed, grad_preact, layer_pattern[0, :, 0], layer_pattern[0, :, 1])
    down_part = block_pairs(hidden, upstream, layer_pattern[1, :, 0], layer_pattern[1, :, 1])
    return jnp.stack([up_part, down_part])


def adam_update(grad_sum, master, moment, variance, token_total):
    gradient = grad_sum / token_total
    moment_next = beta_first * moment + (1.0 - beta_first) * gradient
    variance_next = beta_second * variance + (1.0 - beta_second) * gradient * gradient
    corrected = moment_next / (1.0 - beta_first**update_count)
    spread = jnp.sqrt(variance_next / (1.0 - beta_second**update_count))
    step_direction = corrected / (spread + adam_eps)
    return (step_direction, master - learn_rate * (step_direction + decay_rate * master))


def keep_slot(store, stream, slot_index, active, value):
    previous = store[stream, slot_index]
    return store.at[stream, slot_index].set(jnp.where(active, value, previous))


def shards(tokens, targets, weights, pattern, master, moment, variance):
    section_index = lax.axis_index("section")
    section_count = lax.axis_size("section")
    micro_count = tokens.shape[1]
    row_count = tokens.shape[2]
    tick_count = section_count + micro_count - 1
    local_weights = weights[0]
    local_pattern = pattern[0]
    forward_place = (section_index, section_count - 1 - section_index)
    backward_place = (section_count - 1 - section_index, section_index)

    def stream_forward(stream, tick_index, received, stores):
        slot_raw = tick_index - forward_place[stream]
        active = (slot_raw >= 0) & (slot_raw < micro_count)
        slot_index = jnp.clip(slot_raw, 0, micro_count - 1)
        entering = lax.dynamic_index_in_dim(tokens[stream], slot_index, 0, keepdims=False)
        inputs = jnp.where(forward_place[stream] == 0, entering, received)

        def live_branch(values):
            return layer_forward(values, local_weights[stream], local_pattern[stream])

        def dead_branch(values):
            return (
                jnp.zeros((row_count, D), jnp.bfloat16),
                jnp.zeros((row_count, D), jnp.bfloat16),
                jnp.zeros((row_count, FF), jnp.float32),
                jnp.zeros((row_count, FF), jnp.bfloat16),
            )

        result, normed, preact, hidden = lax.cond(active, live_branch, dead_branch, inputs)
        target_rows = lax.dynamic_index_in_dim(targets[stream], slot_index, 0, keepdims=False)
        residue = (result.astype(jnp.float32) - target_rows.astype(jnp.float32)).astype(
            jnp.bfloat16
        )
        fresh_values = (inputs, normed, preact, hidden, residue)
        stores = tuple(
            (
                keep_slot(store, stream, slot_index, active, value)
                for store, value in zip(stores, fresh_values)
            )
        )
        return (result, stores)

    def forward_tick(state_now, tick_index):
        received_down, received_up, stores = state_now
        result_down, stores = stream_forward(0, tick_index, received_down, stores)
        result_up, stores = stream_forward(1, tick_index, received_up, stores)
        received_down = from_behind(result_down, "section", 1)
        received_up = from_behind(result_up, "section", -1)
        return ((received_down, received_up, stores), None)

    empty_rows = jnp.zeros((row_count, D), jnp.bfloat16)
    forward_stores = (
        jnp.zeros((2, micro_count, row_count, D), jnp.bfloat16),
        jnp.zeros((2, micro_count, row_count, D), jnp.bfloat16),
        jnp.zeros((2, micro_count, row_count, FF), jnp.float32),
        jnp.zeros((2, micro_count, row_count, FF), jnp.bfloat16),
        jnp.zeros((2, micro_count, row_count, D), jnp.bfloat16),
    )
    forward_state, unused = lax.scan(
        forward_tick, (empty_rows, empty_rows, forward_stores), jnp.arange(tick_count)
    )
    saved_inputs, saved_normed, saved_preact, saved_hidden, saved_residue = forward_state[2]

    def stream_backward(stream, tick_index, received, stores):
        slot_raw = tick_index - backward_place[stream]
        active = (slot_raw >= 0) & (slot_raw < micro_count)
        slot_index = jnp.clip(slot_raw, 0, micro_count - 1)
        upstream = jnp.where(
            backward_place[stream] == 0, saved_residue[stream, slot_index], received
        )

        def live_branch(operands):
            return layer_backward(
                operands[0], operands[1], operands[2], local_weights[stream], local_pattern[stream]
            )

        def dead_branch(operands):
            return (
                jnp.zeros((row_count, D), jnp.bfloat16),
                jnp.zeros((row_count, FF), jnp.bfloat16),
            )

        operands = (saved_inputs[stream, slot_index], saved_preact[stream, slot_index], upstream)
        downstream, grad_preact = lax.cond(active, live_branch, dead_branch, operands)
        stores = (
            keep_slot(stores[0], stream, slot_index, active, grad_preact),
            keep_slot(stores[1], stream, slot_index, active, upstream),
        )
        return (downstream, stores)

    def backward_tick(state_now, tick_index):
        received_down, received_up, stores = state_now
        result_down, stores = stream_backward(0, tick_index, received_down, stores)
        result_up, stores = stream_backward(1, tick_index, received_up, stores)
        received_down = from_behind(result_down, "section", -1)
        received_up = from_behind(result_up, "section", 1)
        return ((received_down, received_up, stores), None)

    backward_stores = (
        jnp.zeros((2, micro_count, row_count, FF), jnp.bfloat16),
        jnp.zeros((2, micro_count, row_count, D), jnp.bfloat16),
    )
    backward_state, unused = lax.scan(
        backward_tick, (empty_rows, empty_rows, backward_stores), jnp.arange(tick_count)
    )
    saved_grad_preact, saved_upstream = backward_state[2]

    def copy_grads(stream):
        return weight_grads(
            saved_normed[stream].reshape(-1, D),
            saved_grad_preact[stream].reshape(-1, FF),
            saved_hidden[stream].reshape(-1, FF),
            saved_upstream[stream].reshape(-1, D),
            local_pattern[stream],
        )

    both_grads = jnp.stack([copy_grads(0), copy_grads(1)])
    shares = lax.psum_scatter(
        both_grads.astype(jnp.bfloat16), "dp", scatter_dimension=3, tiled=True
    ).astype(jnp.float32)
    own_share = shares[0]
    other_share = shares[1]
    bit_total = section_count.bit_length() - 1
    bit_order = list(range(bit_total))
    arrived = other_share
    for bit_number in bit_order:
        arrived = partner(arrived.astype(jnp.bfloat16), "section", bit_number).astype(arrived.dtype)
    token_total = 2 * micro_count * row_count * lax.axis_size("dp")
    step_direction, master_next = adam_update(
        own_share + arrived, master[0], moment[0], variance[0], token_total
    )
    return (step_direction[None], master_next[None])


def solution(mesh):
    return jax.shard_map(
        shards,
        mesh=mesh,
        in_specs=(
            P(None, None, "dp", None),
            P(None, None, "dp", None),
            P("section", None, None, None, None, None),
            P("section", None, None, None, None),
            P("section", None, None, "dp", None),
            P("section", None, None, "dp", None),
            P("section", None, None, "dp", None),
        ),
        out_specs=(P("section", None, None, "dp", None), P("section", None, None, "dp", None)),
        check_vma=False,
    )
```

profile of v0, /device:TPU:0, one launch (start us, length us, event | category | flops | bytes accessed | tf_op | source)
XLA Modules:
  0.0 2402.3 jit_solution(15644853176217941906)
XLA Ops:
  25.1 1030.1 %while.54 = (s32[]{:T(128)}, bf16[56,2048]{1,0:T(8,128)(2,1)}, bf16[56,2048]{1,0:T(8,128)(2,1)}, bf16[2,4,56,2048]{3,2,1,0:T(8,128)(2,1)}, bf16[2,4,56,2048]{3,2...) while((s32[]{:T(128)}, bf16[56,2048]{1,0:T(8,128)(2,1)}, ...), condition=%wide.region_13.16_spmd, body=%wide.region_0.15_spmd.sunk | while | flops 735615424 | bytes 153925840 | solution.py:174
  40.8 36.0 %conditional.8 = (bf16[56,2048]{1,0:T(8,128)(2,1)}, bf16[56,2048]{1,0:T(8,128)(2,1)S(1)}, f32[56,8192]{1,0:T(8,128)}, bf16[56,8192]{1,0:T(8,128)(2,1)}, f32[56,2048]{1,0:T(8,128)S(1)}) conditional(s32[]{:T(128)} %convert_element_type.273, () %tuple.241, (bf16[56,2048]{1,0:T(8,128)(2,1)S(1)}, s32[2,2,96,2]{2,3,1,0:T(2,128)S(1)}, ...), branch_computations={%region_1.1_spmd, %region_2.7_spmd} | conditional | flops 364825792 | bytes 48744208 | solution.py:144
  46.5 10.0 scatter_fusion.4
  63.9 10.0 scatter_fusion.5
  121.8 36.1 %conditional.8 = (bf16[56,2048]{1,0:T(8,128)(2,1)}, bf16[56,2048]{1,0:T(8,128)(2,1)S(1)}, f32[56,8192]{1,0:T(8,128)}, bf16[56,8192]{1,0:T(8,128)(2,1)}, f32[56,2048]{1,0:T(8,128)S(1)}) conditional(s32[]{:T(128)} %convert_element_type.273, () %tuple.241, (bf16[56,2048]{1,0:T(8,128)(2,1)S(1)}, s32[2,2,96,2]{2,3,1,0:T(2,128)S(1)}, ...), branch_computations={%region_1.1_spmd, %region_2.7_spmd} | conditional | flops 364825792 | bytes 48744208 | solution.py:144
  127.6 10.0 scatter_fusion.4
  144.9 10.0 scatter_fusion.5
  207.5 36.1 %conditional.8 = (bf16[56,2048]{1,0:T(8,128)(2,1)}, bf16[56,2048]{1,0:T(8,128)(2,1)S(1)}, f32[56,8192]{1,0:T(8,128)}, bf16[56,8192]{1,0:T(8,128)(2,1)}, f32[56,2048]{1,0:T(8,128)S(1)}) conditional(s32[]{:T(128)} %convert_element_type.273, () %tuple.241, (bf16[56,2048]{1,0:T(8,128)(2,1)S(1)}, s32[2,2,96,2]{2,3,1,0:T(2,128)S(1)}, ...), branch_computations={%region_1.1_spmd, %region_2.7_spmd} | conditional | flops 364825792 | bytes 48744208 | solution.py:144
  213.3 10.0 scatter_fusion.4
  230.7 10.0 scatter_fusion.5
  293.4 36.1 %conditional.8 = (bf16[56,2048]{1,0:T(8,128)(2,1)}, bf16[56,2048]{1,0:T(8,128)(2,1)S(1)}, f32[56,8192]{1,0:T(8,128)}, bf16[56,8192]{1,0:T(8,128)(2,1)}, f32[56,2048]{1,0:T(8,128)S(1)}) conditional(s32[]{:T(128)} %convert_element_type.273, () %tuple.241, (bf16[56,2048]{1,0:T(8,128)(2,1)S(1)}, s32[2,2,96,2]{2,3,1,0:T(2,128)S(1)}, ...), branch_computations={%region_1.1_spmd, %region_2.7_spmd} | conditional | flops 364825792 | bytes 48744208 | solution.py:144
  299.1 10.0 scatter_fusion.4
  316.5 10.0 scatter_fusion.5
  382.4 39.6 %collective-permute-start = (bf16[56,2048]{1,0:T(8,128)(2,1)}, bf16[56,2048]{1,0:T(8,128)(2,1)}, u32[]{:S(2)}, u32[]{:S(2)}) collective-permute-start(bf16[56,2048]{1,0:T(8,128)(2,1)} %get-tuple-element.993), channel_id=1, source_target_pairs={{0,16},{16,32},{32,48},{48,64},{64,80},{80,96},{96,112},{1,17},{17... | collective-permute-start | bytes 688136 | tf_op jit(solution)/shard_map/while/body/eval_jaxpr/ppermute | solution.py:24
  515.8 126.7 %collective-permute-start = (bf16[56,2048]{1,0:T(8,128)(2,1)}, bf16[56,2048]{1,0:T(8,128)(2,1)}, u32[]{:S(2)}, u32[]{:S(2)}) collective-permute-start(bf16[56,2048]{1,0:T(8,128)(2,1)} %get-tuple-element.993), channel_id=1, source_target_pairs={{0,16},{16,32},{32,48},{48,64},{64,80},{80,96},{96,112},{1,17},{17... | collective-permute-start | bytes 688136 | tf_op jit(solution)/shard_map/while/body/eval_jaxpr/ppermute | solution.py:24
  677.6 36.3 %conditional.9 = (bf16[56,2048]{1,0:T(8,128)(2,1)}, bf16[56,2048]{1,0:T(8,128)(2,1)S(1)}, f32[56,8192]{1,0:T(8,128)}, bf16[56,8192]{1,0:T(8,128)(2,1)}, f32[56,2048]{1,0:T(8,128)}) conditional(s32[]{:T(128)} %convert_element_type.274, () %tuple.243, (bf16[56,2048]{1,0:T(8,128)(2,1)S(1)}, s32[2,2,96,2]{2,3,1,0:T(2,128)S(1)}, ...), branch_computations={%region_6.8_spmd, %region_7.12_spmd} | conditional | flops 364825792 | bytes 48744208 | solution.py:144
  683.3 10.0 scatter_fusion.6
  700.8 10.0 scatter_fusion.7
  718.3 17.9 collective-permute-start
  774.0 36.3 %conditional.9 = (bf16[56,2048]{1,0:T(8,128)(2,1)}, bf16[56,2048]{1,0:T(8,128)(2,1)S(1)}, f32[56,8192]{1,0:T(8,128)}, bf16[56,8192]{1,0:T(8,128)(2,1)}, f32[56,2048]{1,0:T(8,128)}) conditional(s32[]{:T(128)} %convert_element_type.274, () %tuple.243, (bf16[56,2048]{1,0:T(8,128)(2,1)S(1)}, s32[2,2,96,2]{2,3,1,0:T(2,128)S(1)}, ...), branch_computations={%region_6.8_spmd, %region_7.12_spmd} | conditional | flops 364825792 | bytes 48744208 | solution.py:144
  797.2 10.0 scatter_fusion.7
  814.7 39.6 %collective-permute-start = (bf16[56,2048]{1,0:T(8,128)(2,1)}, bf16[56,2048]{1,0:T(8,128)(2,1)}, u32[]{:S(2)}, u32[]{:S(2)}) collective-permute-start(bf16[56,2048]{1,0:T(8,128)(2,1)} %get-tuple-element.993), channel_id=1, source_target_pairs={{0,16},{16,32},{32,48},{48,64},{64,80},{80,96},{96,112},{1,17},{17... | collective-permute-start | bytes 688136 | tf_op jit(solution)/shard_map/while/body/eval_jaxpr/ppermute | solution.py:24
  892.0 36.3 %conditional.9 = (bf16[56,2048]{1,0:T(8,128)(2,1)}, bf16[56,2048]{1,0:T(8,128)(2,1)S(1)}, f32[56,8192]{1,0:T(8,128)}, bf16[56,8192]{1,0:T(8,128)(2,1)}, f32[56,2048]{1,0:T(8,128)}) conditional(s32[]{:T(128)} %convert_element_type.274, () %tuple.243, (bf16[56,2048]{1,0:T(8,128)(2,1)S(1)}, s32[2,2,96,2]{2,3,1,0:T(2,128)S(1)}, ...), branch_computations={%region_6.8_spmd, %region_7.12_spmd} | conditional | flops 364825792 | bytes 48744208 | solution.py:144
  915.2 10.0 scatter_fusion.7
  932.7 10.0 collective-permute-start
  980.5 36.3 %conditional.9 = (bf16[56,2048]{1,0:T(8,128)(2,1)}, bf16[56,2048]{1,0:T(8,128)(2,1)S(1)}, f32[56,8192]{1,0:T(8,128)}, bf16[56,8192]{1,0:T(8,128)(2,1)}, f32[56,2048]{1,0:T(8,128)}) conditional(s32[]{:T(128)} %convert_element_type.274, () %tuple.243, (bf16[56,2048]{1,0:T(8,128)(2,1)S(1)}, s32[2,2,96,2]{2,3,1,0:T(2,128)S(1)}, ...), branch_computations={%region_6.8_spmd, %region_7.12_spmd} | conditional | flops 364825792 | bytes 48744208 | solution.py:144
  1003.7 10.0 scatter_fusion.7
  1060.1 988.1 %while.55 = (s32[]{:T(128)}, bf16[56,2048]{1,0:T(8,128)(2,1)S(1)}, bf16[56,2048]{1,0:T(8,128)(2,1)}, bf16[2,4,56,8192]{3,2,1,0:T(8,128)(2,1)}, bf16[2,4,56,2048]...) while((s32[]{:T(128)}, bf16[56,2048]{1,0:T(8,128)(2,1)S(1)}, ...), condition=%wide.region_29.33_spmd, body=%wide.region_14.32_spmd.sunk | while | flops 750754432 | bytes 148414816 | solution.py:218
  1080.4 46.6 %conditional.11 = (bf16[56,2048]{1,0:T(8,128)(2,1)}, bf16[56,8192]{1,0:T(8,128)(2,1)}) conditional(s32[]{:T(128)} %convert_element_type.276, () %tuple.251, (bf16[56,2048]{1,0:T(8,128)(2,1)S(1)}, bf16[2,4,56,2048]{3,2,1,0:T(8,128)(2,1)}, s32[]{:T(128)}, s32[2,2,96,2]{2,3,1,0:T(2,128)S(1)}, bf16[2,2,96,128,128]{4,3,2,1,0:T(8,128)(2,1)}, ...), branch_computations={%region_21.24_spmd, %region_22.29_spmd} | conditional | flops 374115616 | bytes 59755372 | solution.py:199
  1087.2 10.0 scatter_fusion.2
  1109.1 10.0 scatter_fusion.3
  1146.8 46.6 %conditional.11 = (bf16[56,2048]{1,0:T(8,128)(2,1)}, bf16[56,8192]{1,0:T(8,128)(2,1)}) conditional(s32[]{:T(128)} %convert_element_type.276, () %tuple.251, (bf16[56,2048]{1,0:T(8,128)(2,1)S(1)}, bf16[2,4,56,2048]{3,2,1,0:T(8,128)(2,1)}, s32[]{:T(128)}, s32[2,2,96,2]{2,3,1,0:T(2,128)S(1)}, bf16[2,2,96,128,128]{4,3,2,1,0:T(8,128)(2,1)}, ...), branch_computations={%region_21.24_spmd, %region_22.29_spmd} | conditional | flops 374115616 | bytes 59755372 | solution.py:199
  1153.6 10.0 scatter_fusion.2
  1175.4 10.0 scatter_fusion.3
  1216.2 46.6 %conditional.11 = (bf16[56,2048]{1,0:T(8,128)(2,1)}, bf16[56,8192]{1,0:T(8,128)(2,1)}) conditional(s32[]{:T(128)} %convert_element_type.276, () %tuple.251, (bf16[56,2048]{1,0:T(8,128)(2,1)S(1)}, bf16[2,4,56,2048]{3,2,1,0:T(8,128)(2,1)}, s32[]{:T(128)}, s32[2,2,96,2]{2,3,1,0:T(2,128)S(1)}, bf16[2,2,96,128,128]{4,3,2,1,0:T(8,128)(2,1)}, ...), branch_computations={%region_21.24_spmd, %region_22.29_spmd} | conditional | flops 374115616 | bytes 59755372 | solution.py:199
  1223.0 10.0 scatter_fusion.2
  1244.8 10.0 scatter_fusion.3
  1286.8 46.6 %conditional.11 = (bf16[56,2048]{1,0:T(8,128)(2,1)}, bf16[56,8192]{1,0:T(8,128)(2,1)}) conditional(s32[]{:T(128)} %convert_element_type.276, () %tuple.251, (bf16[56,2048]{1,0:T(8,128)(2,1)S(1)}, bf16[2,4,56,2048]{3,2,1,0:T(8,128)(2,1)}, s32[]{:T(128)}, s32[2,2,96,2]{2,3,1,0:T(2,128)S(1)}, bf16[2,2,96,128,128]{4,3,2,1,0:T(8,128)(2,1)}, ...), branch_computations={%region_21.24_spmd, %region_22.29_spmd} | conditional | flops 374115616 | bytes 59755372 | solution.py:199
  1293.6 10.0 scatter_fusion.2
  1315.4 10.0 scatter_fusion.3
  1359.1 51.0 %collective-permute-start.3 = (bf16[56,2048]{1,0:T(8,128)(2,1)}, bf16[56,2048]{1,0:T(8,128)(2,1)}, u32[]{:S(2)}, u32[]{:S(2)}) collective-permute-start(bf16[56,2048]{1,0:T(8,128)(2,1)} %get-tuple-element.1033), channel_id=1, source_target_pairs={{0,16},{16,32},{32,48},{48,64},{64,80},{80,96},{96,112},{1,17},{17... | collective-permute-start | bytes 688136 | tf_op jit(solution)/shard_map/while/body/eval_jaxpr/ppermute | solution.py:24
  1429.7 25.5 %collective-permute-start.3 = (bf16[56,2048]{1,0:T(8,128)(2,1)}, bf16[56,2048]{1,0:T(8,128)(2,1)}, u32[]{:S(2)}, u32[]{:S(2)}) collective-permute-start(bf16[56,2048]{1,0:T(8,128)(2,1)} %get-tuple-element.1033), channel_id=1, source_target_pairs={{0,16},{16,32},{32,48},{48,64},{64,80},{80,96},{96,112},{1,17},{17... | collective-permute-start | bytes 688136 | tf_op jit(solution)/shard_map/while/body/eval_jaxpr/ppermute | solution.py:24
  1463.9 90.8 %collective-permute-done.2 = bf16[56,2048]{1,0:T(8,128)(2,1)S(1)} collective-permute-done((bf16[56,2048]{1,0:T(8,128)(2,1)S(1)}, bf16[56,2048]{1,0:T(8,128)(2,1)S(1)}, u32[]{:S(2)}, u32[]{:S(2)}) %collective-permute-start.2) | collective-permute-done | bytes 229408 | tf_op jit(solution)/shard_map/while/body/eval_jaxpr/ppermute | solution.py:24
  1563.8 52.2 %collective-permute-start.3 = (bf16[56,2048]{1,0:T(8,128)(2,1)}, bf16[56,2048]{1,0:T(8,128)(2,1)}, u32[]{:S(2)}, u32[]{:S(2)}) collective-permute-start(bf16[56,2048]{1,0:T(8,128)(2,1)} %get-tuple-element.1033), channel_id=1, source_target_pairs={{0,16},{16,32},{32,48},{48,64},{64,80},{80,96},{96,112},{1,17},{17... | collective-permute-start | bytes 688136 | tf_op jit(solution)/shard_map/while/body/eval_jaxpr/ppermute | solution.py:24
  1624.7 47.2 %collective-permute-done.2 = bf16[56,2048]{1,0:T(8,128)(2,1)S(1)} collective-permute-done((bf16[56,2048]{1,0:T(8,128)(2,1)S(1)}, bf16[56,2048]{1,0:T(8,128)(2,1)S(1)}, u32[]{:S(2)}, u32[]{:S(2)}) %collective-permute-start.2) | collective-permute-done | bytes 229408 | tf_op jit(solution)/shard_map/while/body/eval_jaxpr/ppermute | solution.py:24
  1680.9 51.9 %collective-permute-start.3 = (bf16[56,2048]{1,0:T(8,128)(2,1)}, bf16[56,2048]{1,0:T(8,128)(2,1)}, u32[]{:S(2)}, u32[]{:S(2)}) collective-permute-start(bf16[56,2048]{1,0:T(8,128)(2,1)} %get-tuple-element.1033), channel_id=1, source_target_pairs={{0,16},{16,32},{32,48},{48,64},{64,80},{80,96},{96,112},{1,17},{17... | collective-permute-start | bytes 688136 | tf_op jit(solution)/shard_map/while/body/eval_jaxpr/ppermute | solution.py:24
  1732.8 45.9 %conditional.10 = (bf16[56,2048]{1,0:T(8,128)(2,1)S(1)}, bf16[56,8192]{1,0:T(8,128)(2,1)}) conditional(s32[]{:T(128)} %convert_element_type.275, () %tuple.249, (bf16[56,2048]{1,0:T(8,128)(2,1)S(1)}, bf16[2,4,56,2048]{3,2,1,0:T(8,128)(2,1)}, s32[]{:T(128)}, s32[2,2,96,2]{2,3,1,0:T(2,128)S(1)}, bf16[2,2,96,128,128]{4,3,2,1,0:T(8,128)(2,1)}, ...), branch_computations={%region_15.18_spmd, %region_16.23_spmd} | conditional | flops 374115616 | bytes 59755372 | solution.py:199
  1739.7 10.0 scatter_fusion
  1761.5 10.0 scatter_fusion.1
  1805.0 45.9 %conditional.10 = (bf16[56,2048]{1,0:T(8,128)(2,1)S(1)}, bf16[56,8192]{1,0:T(8,128)(2,1)}) conditional(s32[]{:T(128)} %convert_element_type.275, () %tuple.249, (bf16[56,2048]{1,0:T(8,128)(2,1)S(1)}, bf16[2,4,56,2048]{3,2,1,0:T(8,128)(2,1)}, s32[]{:T(128)}, s32[2,2,96,2]{2,3,1,0:T(2,128)S(1)}, bf16[2,2,96,128,128]{4,3,2,1,0:T(8,128)(2,1)}, ...), branch_computations={%region_15.18_spmd, %region_16.23_spmd} | conditional | flops 374115616 | bytes 59755372 | solution.py:199
  1811.8 10.0 scatter_fusion
  1833.6 10.0 scatter_fusion.1
  1859.6 45.7 %collective-permute-done.2 = bf16[56,2048]{1,0:T(8,128)(2,1)S(1)} collective-permute-done((bf16[56,2048]{1,0:T(8,128)(2,1)S(1)}, bf16[56,2048]{1,0:T(8,128)(2,1)S(1)}, u32[]{:S(2)}, u32[]{:S(2)}) %collective-permute-start.2) | collective-permute-done | bytes 229408 | tf_op jit(solution)/shard_map/while/body/eval_jaxpr/ppermute | solution.py:24
  1921.5 45.9 %conditional.10 = (bf16[56,2048]{1,0:T(8,128)(2,1)S(1)}, bf16[56,8192]{1,0:T(8,128)(2,1)}) conditional(s32[]{:T(128)} %convert_element_type.275, () %tuple.249, (bf16[56,2048]{1,0:T(8,128)(2,1)S(1)}, bf16[2,4,56,2048]{3,2,1,0:T(8,128)(2,1)}, s32[]{:T(128)}, s32[2,2,96,2]{2,3,1,0:T(2,128)S(1)}, bf16[2,2,96,128,128]{4,3,2,1,0:T(8,128)(2,1)}, ...), branch_computations={%region_15.18_spmd, %region_16.23_spmd} | conditional | flops 374115616 | bytes 59755372 | solution.py:199
  1928.4 10.0 scatter_fusion
  1950.2 10.0 scatter_fusion.1
  1992.5 45.9 %conditional.10 = (bf16[56,2048]{1,0:T(8,128)(2,1)S(1)}, bf16[56,8192]{1,0:T(8,128)(2,1)}) conditional(s32[]{:T(128)} %convert_element_type.275, () %tuple.249, (bf16[56,2048]{1,0:T(8,128)(2,1)S(1)}, bf16[2,4,56,2048]{3,2,1,0:T(8,128)(2,1)}, s32[]{:T(128)}, s32[2,2,96,2]{2,3,1,0:T(2,128)S(1)}, bf16[2,2,96,128,128]{4,3,2,1,0:T(8,128)(2,1)}, ...), branch_computations={%region_15.18_spmd, %region_16.23_spmd} | conditional | flops 374115616 | bytes 59755372 | solution.py:199
  1999.3 10.0 scatter_fusion
  2021.1 10.0 scatter_fusion.1
  2164.8 27.4 %copy.81 = bf16[2,2,96,128,128]{4,2,1,0,3:T(8,128)(2,1)S(1)} copy(bf16[2,2,96,128,128]{4,3,2,1,0:T(8,128)(2,1)S(1)} %pad_maximum_fusion) | data formatting | bytes 25165824
  2192.2 27.9 %copy.137 = bf16[16,8,384,128]{3,1,2,0:T(8,128)(2,1)} copy(bf16[16,8,384,128]{3,2,1,0:T(8,128)(2,1)S(1)} %bitcast.666) | data formatting | bytes 25165824
  2220.1 135.1 %reduce-scatter.4.cloned.1.call-done = bf16[8,49152]{1,0:T(8,128)(2,1)} async-done(((bf16[128,49152]{1,0:T(8,128)(2,1)}), bf16[8,49152]{1,0:T(8,128)(2,1)}) %reduce-scatter.4.cloned.1.call-update) | async-done | bytes 786448
  2369.3 10.8 collective-permute-done.5
  2381.7 11.4 collective-permute-done.6
  (1141 shorter events, 1310.2 us)
Async XLA Ops:
  7.2 2348.1 %reduce-scatter.4.cloned.1.call-start = ((), (), s32[]{:S(2)}) async-start(), calls=%async_computation.1 | async-start | bytes 13369344
  39.4 66.7 %collective-permute-start.1 = (bf16[56,2048]{1,0:T(8,128)(2,1)}, bf16[56,2048]{1,0:T(8,128)(2,1)}, u32[]{:S(2)}, u32[]{:S(2)}) collective-permute-start(bf16[56,2048]{1,0:T(8,128)(2,1)} %get-tuple-element.998), channel_id=1, source_target_pairs={{16,0},{32,16},{48,32},{64,48},{80,64},{96,80},{112,96},{17,1},{33... | collective-permute-start | bytes 688136 | tf_op jit(solution)/shard_map/while/body/eval_jaxpr/ppermute | solution.py:24
  76.8 29.3 %collective-permute-start = (bf16[56,2048]{1,0:T(8,128)(2,1)}, bf16[56,2048]{1,0:T(8,128)(2,1)}, u32[]{:S(2)}, u32[]{:S(2)}) collective-permute-start(bf16[56,2048]{1,0:T(8,128)(2,1)} %get-tuple-element.993), channel_id=1, source_target_pairs={{0,16},{16,32},{32,48},{48,64},{64,80},{80,96},{96,112},{1,17},{17... | collective-permute-start | bytes 688136 | tf_op jit(solution)/shard_map/while/body/eval_jaxpr/ppermute | solution.py:24
  120.5 71.4 %collective-permute-start.1 = (bf16[56,2048]{1,0:T(8,128)(2,1)}, bf16[56,2048]{1,0:T(8,128)(2,1)}, u32[]{:S(2)}, u32[]{:S(2)}) collective-permute-start(bf16[56,2048]{1,0:T(8,128)(2,1)} %get-tuple-element.998), channel_id=1, source_target_pairs={{16,0},{32,16},{48,32},{64,48},{80,64},{96,80},{112,96},{17,1},{33... | collective-permute-start | bytes 688136 | tf_op jit(solution)/shard_map/while/body/eval_jaxpr/ppermute | solution.py:24
  157.8 8.7 copy-start.6
  157.8 34.1 %collective-permute-start = (bf16[56,2048]{1,0:T(8,128)(2,1)}, bf16[56,2048]{1,0:T(8,128)(2,1)}, u32[]{:S(2)}, u32[]{:S(2)}) collective-permute-start(bf16[56,2048]{1,0:T(8,128)(2,1)} %get-tuple-element.993), channel_id=1, source_target_pairs={{0,16},{16,32},{32,48},{48,64},{64,80},{80,96},{96,112},{1,17},{17... | collective-permute-start | bytes 688136 | tf_op jit(solution)/shard_map/while/body/eval_jaxpr/ppermute | solution.py:24
  206.2 71.5 %collective-permute-start.1 = (bf16[56,2048]{1,0:T(8,128)(2,1)}, bf16[56,2048]{1,0:T(8,128)(2,1)}, u32[]{:S(2)}, u32[]{:S(2)}) collective-permute-start(bf16[56,2048]{1,0:T(8,128)(2,1)} %get-tuple-element.998), channel_id=1, source_target_pairs={{16,0},{32,16},{48,32},{64,48},{80,64},{96,80},{112,96},{17,1},{33... | collective-permute-start | bytes 688136 | tf_op jit(solution)/shard_map/while/body/eval_jaxpr/ppermute | solution.py:24
  243.6 34.1 %collective-permute-start = (bf16[56,2048]{1,0:T(8,128)(2,1)}, bf16[56,2048]{1,0:T(8,128)(2,1)}, u32[]{:S(2)}, u32[]{:S(2)}) collective-permute-start(bf16[56,2048]{1,0:T(8,128)(2,1)} %get-tuple-element.993), channel_id=1, source_target_pairs={{0,16},{16,32},{32,48},{48,64},{64,80},{80,96},{96,112},{1,17},{17... | collective-permute-start | bytes 688136 | tf_op jit(solution)/shard_map/while/body/eval_jaxpr/ppermute | solution.py:24
  292.0 71.5 %collective-permute-start.1 = (bf16[56,2048]{1,0:T(8,128)(2,1)}, bf16[56,2048]{1,0:T(8,128)(2,1)}, u32[]{:S(2)}, u32[]{:S(2)}) collective-permute-start(bf16[56,2048]{1,0:T(8,128)(2,1)} %get-tuple-element.998), channel_id=1, source_target_pairs={{16,0},{32,16},{48,32},{64,48},{80,64},{96,80},{112,96},{17,1},{33... | collective-permute-start | bytes 688136 | tf_op jit(solution)/shard_map/while/body/eval_jaxpr/ppermute | solution.py:24
  329.4 34.1 %collective-permute-start = (bf16[56,2048]{1,0:T(8,128)(2,1)}, bf16[56,2048]{1,0:T(8,128)(2,1)}, u32[]{:S(2)}, u32[]{:S(2)}) collective-permute-start(bf16[56,2048]{1,0:T(8,128)(2,1)} %get-tuple-element.993), channel_id=1, source_target_pairs={{0,16},{16,32},{32,48},{48,64},{64,80},{80,96},{96,112},{1,17},{17... | collective-permute-start | bytes 688136 | tf_op jit(solution)/shard_map/while/body/eval_jaxpr/ppermute | solution.py:24
  377.9 68.9 %collective-permute-start.1 = (bf16[56,2048]{1,0:T(8,128)(2,1)}, bf16[56,2048]{1,0:T(8,128)(2,1)}, u32[]{:S(2)}, u32[]{:S(2)}) collective-permute-start(bf16[56,2048]{1,0:T(8,128)(2,1)} %get-tuple-element.998), channel_id=1, source_target_pairs={{16,0},{32,16},{48,32},{64,48},{80,64},{96,80},{112,96},{17,1},{33... | collective-permute-start | bytes 688136 | tf_op jit(solution)/shard_map/while/body/eval_jaxpr/ppermute | solution.py:24
  382.4 41.6 %copy-start.6 = (bf16[56,2048]{1,0:T(8,128)(2,1)}, bf16[56,2048]{1,0:T(8,128)(2,1)S(1)}, u32[]{:S(2)}) copy-start(bf16[56,2048]{1,0:T(8,128)(2,1)S(1)} %get-tuple-element.1002) | copy-start | bytes 688132 | tf_op jit(solution)/shard_map/while
  382.4 64.4 %collective-permute-start = (bf16[56,2048]{1,0:T(8,128)(2,1)}, bf16[56,2048]{1,0:T(8,128)(2,1)}, u32[]{:S(2)}, u32[]{:S(2)}) collective-permute-start(bf16[56,2048]{1,0:T(8,128)(2,1)} %get-tuple-element.993), channel_id=1, source_target_pairs={{0,16},{16,32},{32,48},{48,64},{64,80},{80,96},{96,112},{1,17},{17... | collective-permute-start | bytes 688136 | tf_op jit(solution)/shard_map/while/body/eval_jaxpr/ppermute | solution.py:24
  461.1 36.0 %collective-permute-start.1 = (bf16[56,2048]{1,0:T(8,128)(2,1)}, bf16[56,2048]{1,0:T(8,128)(2,1)}, u32[]{:S(2)}, u32[]{:S(2)}) collective-permute-start(bf16[56,2048]{1,0:T(8,128)(2,1)} %get-tuple-element.998), channel_id=1, source_target_pairs={{16,0},{32,16},{48,32},{64,48},{80,64},{96,80},{112,96},{17,1},{33... | collective-permute-start | bytes 688136 | tf_op jit(solution)/shard_map/while/body/eval_jaxpr/ppermute | solution.py:24
  465.5 31.5 %collective-permute-start = (bf16[56,2048]{1,0:T(8,128)(2,1)}, bf16[56,2048]{1,0:T(8,128)(2,1)}, u32[]{:S(2)}, u32[]{:S(2)}) collective-permute-start(bf16[56,2048]{1,0:T(8,128)(2,1)} %get-tuple-element.993), channel_id=1, source_target_pairs={{0,16},{16,32},{32,48},{48,64},{64,80},{80,96},{96,112},{1,17},{17... | collective-permute-start | bytes 688136 | tf_op jit(solution)/shard_map/while/body/eval_jaxpr/ppermute | solution.py:24
  511.3 155.9 %collective-permute-start.1 = (bf16[56,2048]{1,0:T(8,128)(2,1)}, bf16[56,2048]{1,0:T(8,128)(2,1)}, u32[]{:S(2)}, u32[]{:S(2)}) collective-permute-start(bf16[56,2048]{1,0:T(8,128)(2,1)} %get-tuple-element.998), channel_id=1, source_target_pairs={{16,0},{32,16},{48,32},{64,48},{80,64},{96,80},{112,96},{17,1},{33... | collective-permute-start | bytes 688136 | tf_op jit(solution)/shard_map/while/body/eval_jaxpr/ppermute | solution.py:24
  515.8 128.6 %copy-start.6 = (bf16[56,2048]{1,0:T(8,128)(2,1)}, bf16[56,2048]{1,0:T(8,128)(2,1)S(1)}, u32[]{:S(2)}) copy-start(bf16[56,2048]{1,0:T(8,128)(2,1)S(1)} %get-tuple-element.1002) | copy-start | bytes 688132 | tf_op jit(solution)/shard_map/while
  515.8 151.4 %collective-permute-start = (bf16[56,2048]{1,0:T(8,128)(2,1)}, bf16[56,2048]{1,0:T(8,128)(2,1)}, u32[]{:S(2)}, u32[]{:S(2)}) collective-permute-start(bf16[56,2048]{1,0:T(8,128)(2,1)} %get-tuple-element.993), channel_id=1, source_target_pairs={{0,16},{16,32},{32,48},{48,64},{64,80},{80,96},{96,112},{1,17},{17... | collective-permute-start | bytes 688136 | tf_op jit(solution)/shard_map/while/body/eval_jaxpr/ppermute | solution.py:24
  713.8 49.8 %collective-permute-start.1 = (bf16[56,2048]{1,0:T(8,128)(2,1)}, bf16[56,2048]{1,0:T(8,128)(2,1)}, u32[]{:S(2)}, u32[]{:S(2)}) collective-permute-start(bf16[56,2048]{1,0:T(8,128)(2,1)} %get-tuple-element.998), channel_id=1, source_target_pairs={{16,0},{32,16},{48,32},{64,48},{80,64},{96,80},{112,96},{17,1},{33... | collective-permute-start | bytes 688136 | tf_op jit(solution)/shard_map/while/body/eval_jaxpr/ppermute | solution.py:24
  718.3 19.9 copy-start.6
  718.3 45.3 %collective-permute-start = (bf16[56,2048]{1,0:T(8,128)(2,1)}, bf16[56,2048]{1,0:T(8,128)(2,1)}, u32[]{:S(2)}, u32[]{:S(2)}) collective-permute-start(bf16[56,2048]{1,0:T(8,128)(2,1)} %get-tuple-element.993), channel_id=1, source_target_pairs={{0,16},{16,32},{32,48},{48,64},{64,80},{80,96},{96,112},{1,17},{17... | collective-permute-start | bytes 688136 | tf_op jit(solution)/shard_map/while/body/eval_jaxpr/ppermute | solution.py:24
  810.3 71.4 %collective-permute-start.1 = (bf16[56,2048]{1,0:T(8,128)(2,1)}, bf16[56,2048]{1,0:T(8,128)(2,1)}, u32[]{:S(2)}, u32[]{:S(2)}) collective-permute-start(bf16[56,2048]{1,0:T(8,128)(2,1)} %get-tuple-element.998), channel_id=1, source_target_pairs={{16,0},{32,16},{48,32},{64,48},{80,64},{96,80},{112,96},{17,1},{33... | collective-permute-start | bytes 688136 | tf_op jit(solution)/shard_map/while/body/eval_jaxpr/ppermute | solution.py:24
  814.7 41.5 %copy-start.6 = (bf16[56,2048]{1,0:T(8,128)(2,1)}, bf16[56,2048]{1,0:T(8,128)(2,1)S(1)}, u32[]{:S(2)}) copy-start(bf16[56,2048]{1,0:T(8,128)(2,1)S(1)} %get-tuple-element.1002) | copy-start | bytes 688132 | tf_op jit(solution)/shard_map/while
  814.7 66.9 %collective-permute-start = (bf16[56,2048]{1,0:T(8,128)(2,1)}, bf16[56,2048]{1,0:T(8,128)(2,1)}, u32[]{:S(2)}, u32[]{:S(2)}) collective-permute-start(bf16[56,2048]{1,0:T(8,128)(2,1)} %get-tuple-element.993), channel_id=1, source_target_pairs={{0,16},{16,32},{32,48},{48,64},{64,80},{80,96},{96,112},{1,17},{17... | collective-permute-start | bytes 688136 | tf_op jit(solution)/shard_map/while/body/eval_jaxpr/ppermute | solution.py:24
  928.2 41.9 %collective-permute-start.1 = (bf16[56,2048]{1,0:T(8,128)(2,1)}, bf16[56,2048]{1,0:T(8,128)(2,1)}, u32[]{:S(2)}, u32[]{:S(2)}) collective-permute-start(bf16[56,2048]{1,0:T(8,128)(2,1)} %get-tuple-element.998), channel_id=1, source_target_pairs={{16,0},{32,16},{48,32},{64,48},{80,64},{96,80},{112,96},{17,1},{33... | collective-permute-start | bytes 688136 | tf_op jit(solution)/shard_map/while/body/eval_jaxpr/ppermute | solution.py:24
  932.7 12.0 copy-start.6
  932.7 37.4 %collective-permute-start = (bf16[56,2048]{1,0:T(8,128)(2,1)}, bf16[56,2048]{1,0:T(8,128)(2,1)}, u32[]{:S(2)}, u32[]{:S(2)}) collective-permute-start(bf16[56,2048]{1,0:T(8,128)(2,1)} %get-tuple-element.993), channel_id=1, source_target_pairs={{0,16},{16,32},{32,48},{48,64},{64,80},{80,96},{96,112},{1,17},{17... | collective-permute-start | bytes 688136 | tf_op jit(solution)/shard_map/while/body/eval_jaxpr/ppermute | solution.py:24
  1016.8 38.5 %collective-permute-start.1 = (bf16[56,2048]{1,0:T(8,128)(2,1)}, bf16[56,2048]{1,0:T(8,128)(2,1)}, u32[]{:S(2)}, u32[]{:S(2)}) collective-permute-start(bf16[56,2048]{1,0:T(8,128)(2,1)} %get-tuple-element.998), channel_id=1, source_target_pairs={{16,0},{32,16},{48,32},{64,48},{80,64},{96,80},{112,96},{17,1},{33... | collective-permute-start | bytes 688136 | tf_op jit(solution)/shard_map/while/body/eval_jaxpr/ppermute | solution.py:24
  1021.2 34.0 %collective-permute-start = (bf16[56,2048]{1,0:T(8,128)(2,1)}, bf16[56,2048]{1,0:T(8,128)(2,1)}, u32[]{:S(2)}, u32[]{:S(2)}) collective-permute-start(bf16[56,2048]{1,0:T(8,128)(2,1)} %get-tuple-element.993), channel_id=1, source_target_pairs={{0,16},{16,32},{32,48},{48,64},{64,80},{80,96},{96,112},{1,17},{17... | collective-permute-start | bytes 688136 | tf_op jit(solution)/shard_map/while/body/eval_jaxpr/ppermute | solution.py:24
  1127.0 11.8 collective-permute-start.3
  1130.0 9.4 collective-permute-start.2
  1193.4 14.9 collective-permute-start.3
  1199.5 9.4 collective-permute-start.2
  1262.8 16.0 collective-permute-start.3
  1270.0 9.4 collective-permute-start.2
  1333.4 16.1 collective-permute-start.3
  1340.6 9.4 collective-permute-start.2
  1359.1 59.7 %collective-permute-start.3 = (bf16[56,2048]{1,0:T(8,128)(2,1)}, bf16[56,2048]{1,0:T(8,128)(2,1)}, u32[]{:S(2)}, u32[]{:S(2)}) collective-permute-start(bf16[56,2048]{1,0:T(8,128)(2,1)} %get-tuple-element.1033), channel_id=1, source_target_pairs={{0,16},{16,32},{32,48},{48,64},{64,80},{80,96},{96,112},{1,17},{17... | collective-permute-start | bytes 688136 | tf_op jit(solution)/shard_map/while/body/eval_jaxpr/ppermute | solution.py:24
  1411.2 9.4 collective-permute-start.2
  1429.7 34.2 %collective-permute-start.3 = (bf16[56,2048]{1,0:T(8,128)(2,1)}, bf16[56,2048]{1,0:T(8,128)(2,1)}, u32[]{:S(2)}, u32[]{:S(2)}) collective-permute-start(bf16[56,2048]{1,0:T(8,128)(2,1)} %get-tuple-element.1033), channel_id=1, source_target_pairs={{0,16},{16,32},{32,48},{48,64},{64,80},{80,96},{96,112},{1,17},{17... | collective-permute-start | bytes 688136 | tf_op jit(solution)/shard_map/while/body/eval_jaxpr/ppermute | solution.py:24
  1456.3 98.4 %collective-permute-start.2 = (bf16[56,2048]{1,0:T(8,128)(2,1)S(1)}, bf16[56,2048]{1,0:T(8,128)(2,1)S(1)}, u32[]{:S(2)}, u32[]{:S(2)}) collective-permute-start(bf16[56,2048]{1,0:T(8,128)(2,1)S(1)} %get-tuple-element.1029), channel_id=1, source_target_pairs={{16,0},{32,16},{48,32},{64,48},{80,64},{96,80},{112,96},{17,1},{33... | collective-permute-start | bytes 688136 | tf_op jit(solution)/shard_map/while/body/eval_jaxpr/ppermute | solution.py:24
  1461.9 92.8 %copy-start.9 = (bf16[2,4,56,2048]{3,2,1,0:T(8,128)(2,1)S(1)}, bf16[2,4,56,2048]{3,2,1,0:T(8,128)(2,1)}, u32[]{:S(2)}) copy-start(bf16[2,4,56,2048]{3,2,1,0:T(8,128)(2,1)} %copy-done.8) | copy-start | bytes 5505028 | tf_op jit(solution)/shard_map/while
  1563.8 60.9 %collective-permute-start.3 = (bf16[56,2048]{1,0:T(8,128)(2,1)}, bf16[56,2048]{1,0:T(8,128)(2,1)}, u32[]{:S(2)}, u32[]{:S(2)}) collective-permute-start(bf16[56,2048]{1,0:T(8,128)(2,1)} %get-tuple-element.1033), channel_id=1, source_target_pairs={{0,16},{16,32},{32,48},{48,64},{64,80},{80,96},{96,112},{1,17},{17... | collective-permute-start | bytes 688136 | tf_op jit(solution)/shard_map/while/body/eval_jaxpr/ppermute | solution.py:24
  1617.1 54.8 %collective-permute-start.2 = (bf16[56,2048]{1,0:T(8,128)(2,1)S(1)}, bf16[56,2048]{1,0:T(8,128)(2,1)S(1)}, u32[]{:S(2)}, u32[]{:S(2)}) collective-permute-start(bf16[56,2048]{1,0:T(8,128)(2,1)S(1)} %get-tuple-element.1029), channel_id=1, source_target_pairs={{16,0},{32,16},{48,32},{64,48},{80,64},{96,80},{112,96},{17,1},{33... | collective-permute-start | bytes 688136 | tf_op jit(solution)/shard_map/while/body/eval_jaxpr/ppermute | solution.py:24
  1622.7 49.2 %copy-start.9 = (bf16[2,4,56,2048]{3,2,1,0:T(8,128)(2,1)S(1)}, bf16[2,4,56,2048]{3,2,1,0:T(8,128)(2,1)}, u32[]{:S(2)}) copy-start(bf16[2,4,56,2048]{3,2,1,0:T(8,128)(2,1)} %copy-done.8) | copy-start | bytes 5505028 | tf_op jit(solution)/shard_map/while
  1680.9 106.6 %collective-permute-start.3 = (bf16[56,2048]{1,0:T(8,128)(2,1)}, bf16[56,2048]{1,0:T(8,128)(2,1)}, u32[]{:S(2)}, u32[]{:S(2)}) collective-permute-start(bf16[56,2048]{1,0:T(8,128)(2,1)} %get-tuple-element.1033), channel_id=1, source_target_pairs={{0,16},{16,32},{32,48},{48,64},{64,80},{80,96},{96,112},{1,17},{17... | collective-permute-start | bytes 688136 | tf_op jit(solution)/shard_map/while/body/eval_jaxpr/ppermute | solution.py:24
  1778.7 9.7 collective-permute-start.2
  1797.5 62.1 %collective-permute-start.3 = (bf16[56,2048]{1,0:T(8,128)(2,1)}, bf16[56,2048]{1,0:T(8,128)(2,1)}, u32[]{:S(2)}, u32[]{:S(2)}) collective-permute-start(bf16[56,2048]{1,0:T(8,128)(2,1)} %get-tuple-element.1033), channel_id=1, source_target_pairs={{0,16},{16,32},{32,48},{48,64},{64,80},{80,96},{96,112},{1,17},{17... | collective-permute-start | bytes 688136 | tf_op jit(solution)/shard_map/while/body/eval_jaxpr/ppermute | solution.py:24
  1850.9 54.5 %collective-permute-start.2 = (bf16[56,2048]{1,0:T(8,128)(2,1)S(1)}, bf16[56,2048]{1,0:T(8,128)(2,1)S(1)}, u32[]{:S(2)}, u32[]{:S(2)}) collective-permute-start(bf16[56,2048]{1,0:T(8,128)(2,1)S(1)} %get-tuple-element.1029), channel_id=1, source_target_pairs={{16,0},{32,16},{48,32},{64,48},{80,64},{96,80},{112,96},{17,1},{33... | collective-permute-start | bytes 688136 | tf_op jit(solution)/shard_map/while/body/eval_jaxpr/ppermute | solution.py:24
  1857.6 47.7 %copy-start.9 = (bf16[2,4,56,2048]{3,2,1,0:T(8,128)(2,1)S(1)}, bf16[2,4,56,2048]{3,2,1,0:T(8,128)(2,1)}, u32[]{:S(2)}) copy-start(bf16[2,4,56,2048]{3,2,1,0:T(8,128)(2,1)} %copy-done.8) | copy-start | bytes 5505028 | tf_op jit(solution)/shard_map/while
  1914.4 61.8 %collective-permute-start.3 = (bf16[56,2048]{1,0:T(8,128)(2,1)}, bf16[56,2048]{1,0:T(8,128)(2,1)}, u32[]{:S(2)}, u32[]{:S(2)}) collective-permute-start(bf16[56,2048]{1,0:T(8,128)(2,1)} %get-tuple-element.1033), channel_id=1, source_target_pairs={{0,16},{16,32},{32,48},{48,64},{64,80},{80,96},{96,112},{1,17},{17... | collective-permute-start | bytes 688136 | tf_op jit(solution)/shard_map/while/body/eval_jaxpr/ppermute | solution.py:24
  1967.4 9.4 collective-permute-start.2
  1985.9 61.3 %collective-permute-start.3 = (bf16[56,2048]{1,0:T(8,128)(2,1)}, bf16[56,2048]{1,0:T(8,128)(2,1)}, u32[]{:S(2)}, u32[]{:S(2)}) collective-permute-start(bf16[56,2048]{1,0:T(8,128)(2,1)} %get-tuple-element.1033), channel_id=1, source_target_pairs={{0,16},{16,32},{32,48},{48,64},{64,80},{80,96},{96,112},{1,17},{17... | collective-permute-start | bytes 688136 | tf_op jit(solution)/shard_map/while/body/eval_jaxpr/ppermute | solution.py:24
  2038.4 9.4 collective-permute-start.2
  2051.3 9.9 slice-start
  2139.0 14.3 slice-start.4
  2145.0 18.5 slice-start.2
  2153.4 10.1 slice-start.3
  2355.3 37.8 %copy-start.12 = (f32[1,2,96,8,128]{4,3,2,1,0:T(8,128)S(1)}, f32[1,2,96,8,128]{4,3,2,1,0:T(8,128)}, u32[]{:S(2)}) copy-start(f32[1,2,96,8,128]{4,3,2,1,0:T(8,128)} %param.59) | copy-start | bytes 2359300
  2355.3 37.8 %copy-start.13 = (f32[1,2,96,8,128]{4,3,2,1,0:T(8,128)S(1)}, f32[1,2,96,8,128]{4,3,2,1,0:T(8,128)}, u32[]{:S(2)}) copy-start(f32[1,2,96,8,128]{4,3,2,1,0:T(8,128)} %param.61) | copy-start | bytes 2359300
  2355.3 37.8 %copy-start.14 = (f32[1,2,96,8,128]{4,3,2,1,0:T(8,128)S(1)}, f32[1,2,96,8,128]{4,3,2,1,0:T(8,128)}, u32[]{:S(2)}) copy-start(f32[1,2,96,8,128]{4,3,2,1,0:T(8,128)} %param.60) | copy-start | bytes 2359300
  2357.0 11.8 collective-permute-start.4
  2368.7 11.4 collective-permute-start.5
  2380.1 13.0 collective-permute-start.6
  (79 other events, 282.8 us)
Sparse Core Ops, SparseCore 0:
  2220.2 134.9 reduce-scatter.3
where the time goes:
time: 2440 us; the launch traced here: 2400 us
  other arithmetic  761 us (31%)
  starting transfers between devices  524 us (21%)
  local copies, waits for them, and re-layouts  501 us (21%)
  waiting for transfers between devices  357 us (15%)
  matrix products  198 us (8%)
  loops' own time  46.1 us (2%)
    ppermute x44, starting transfers between devices, from_behind(): return lax.ppermute(x, axis, pairs)  519 us
    scatter x143, other arithmetic, keep_slot(): return store.at[stream, slot_index].set(jnp.where(active, value, previous))  309 us
    ppermute x44, waiting for transfers between devices, from_behind(): return lax.ppermute(x, axis, pairs)  190 us
    scatter-add x16, other arithmetic, sparse_transposed(): summed = jax.ops.segment_sum(product, put_index, num_segments=out_blocks)  160 us
    scatter-add x16, other arithmetic, sparse_product(): summed = jax.ops.segment_sum(product, put_index, num_segments=out_blocks)  160 us
    dynamic_slice x154, local copies, waits for them, and re-layouts, keep_slot(): previous = store[stream, slot_index]  154 us
    unnamed x2, waiting for transfers between devices  135 us
    dot_general x16, matrix products, sparse_transposed(): jnp.einsum('rkb,kab->kra', picked, blocks, preferred_element_type=jnp.flo...  95.4 us
  transfers between devices with their start and end apart: 48, of which 15 were waited for; matrix products, arithmetic and copies ran while one was open for 30% of the time, Pallas kernels for 0%

commit v1 on v0

v1 whole, which is shorter than its diff:
```python
import functools

import jax
import jax.numpy as jnp
from jax import lax
from jax.experimental import pallas as pl
from jax.experimental.pallas import tpu as pltpu
from jax.sharding import PartitionSpec as P

D = 2048
FF = 8192
BS = 128
NNZ = 96
DB = D // BS
FB = FF // BS
STAGES = 4
ROWS = 32
UNROLL = 48

norm_eps = 1e-06
gelu_coef = 0.7978845608028654
beta_first = 0.9
beta_second = 0.95
adam_eps = 1e-08
learn_rate = 0.001
decay_rate = 0.1
update_count = 10

MESH = pl.DeviceIdType.MESH
f32 = jnp.float32
bf16 = jnp.bfloat16

UPF_ROW, UPF_PERM, UP_LAST = 0, 96, 192
DNF_ROW, DNF_PERM, DN_LAST = 256, 352, 448
VB_COL, VB_LAST = 464, 560
UB_COL, UB_LAST = 624, 720
U_ROW, V_ROW = 736, 832
TABLE = 928
K_UPF, K_DNF, K_VB, K_UB, KEEPS = 0, 96, 192, 288, 384


def make_orders(chunks, cost_forward, cost_backward, hop):
    arrival = {(0, 0, c): 0.0 for c in range(chunks)}
    free = [0.0] * STAGES
    orders = [[] for _ in range(STAGES)]
    for _ in range(4 * STAGES * chunks):
        start, later, chunk, stage = min(
            (max(t, free[s]), -op, c, s) for (s, op, c), t in arrival.items()
        )
        op = -later
        del arrival[(stage, op, chunk)]
        end = start + (cost_forward if op < 2 else cost_backward)
        free[stage] = end
        orders[stage].append(op * chunks + chunk)
        following = stage + (1 if op % 2 == 0 else -1)
        if 0 <= following < STAGES:
            arrival[(following, op, chunk)] = end + hop
        elif op < 3:
            arrival[(stage, op + 1, chunk)] = end
    return orders


def tables(pattern):
    rows, cols = pattern[..., 0], pattern[..., 1]
    key = cols * 64 + rows
    rank = jnp.sum((key[..., None, :] < key[..., :, None]).astype(jnp.int32), axis=-1)
    slots = jnp.arange(NNZ, dtype=jnp.int32)
    hit = (rank[..., None, :] == slots[:, None]).astype(jnp.int32)
    perm = jnp.sum(hit * slots, axis=-1)
    sorted_rows = jnp.sum(hit * rows[..., None, :], axis=-1)
    sorted_cols = jnp.sum(hit * cols[..., None, :], axis=-1)

    def last(values, count):
        bins = jnp.arange(count, dtype=jnp.int32)[:, None]
        through = jnp.sum((values[..., None, :] <= bins).astype(jnp.int32), axis=-1)
        here = jnp.sum((values[..., None, :] == bins).astype(jnp.int32), axis=-1)
        return jnp.where(here > 0, through - 1, NNZ)

    def keep(values):
        same = (values[..., 1:] == values[..., :-1]).astype(f32)
        return jnp.concatenate([jnp.zeros_like(same[..., :1]), same], axis=-1)

    index = jnp.concatenate(
        [
            sorted_rows[:, 0],
            perm[:, 0],
            last(cols[:, 0], FB),
            sorted_rows[:, 1],
            perm[:, 1],
            last(cols[:, 1], DB),
            cols[:, 1],
            last(rows[:, 1], FB),
            cols[:, 0],
            last(rows[:, 0], DB),
            rows[:, 0],
            rows[:, 1],
        ],
        axis=-1,
    )
    keeps = jnp.concatenate(
        [keep(sorted_cols[:, 0]), keep(sorted_cols[:, 1]), keep(rows[:, 1]), keep(rows[:, 0])],
        axis=-1,
    )
    return index.reshape(-1), keeps.reshape(-1)


def pick(stage, values):
    out = jnp.int32(values[0])
    for s in range(1, STAGES):
        out = jnp.where(stage == s, jnp.int32(values[s]), out)
    return out


def pipeline_kernel(
    chunks,
    orders,
    tab,
    keeps,
    tok,
    tgt,
    wts,
    grads,
    W,
    WT,
    ACT,
    OUT,
    COT,
    NORM,
    H,
    S,
    TG,
    PS,
    w_sem,
    t_sem,
    send_sem,
    recv_sem,
):
    R = ROWS
    total_rows = chunks * R
    section = lax.axis_index("section")
    dp = lax.axis_index("dp")
    x, z_hi = section // 2, section % 2
    stage = jnp.where(section < 4, section, 7 - section)
    own = jnp.where(section < 4, 0, 1)

    def section_of(s):
        return jnp.where(s % 2 == z_hi, s, 7 - s)

    upper = section_of(stage + 1)
    lower = section_of(stage - 1)

    barrier = pltpu.get_barrier_semaphore()

    @pl.when(stage < STAGES - 1)
    def _():
        pl.semaphore_signal(barrier, inc=1, device_id=(upper, dp), device_id_type=MESH)

    @pl.when(stage > 0)
    def _():
        pl.semaphore_signal(barrier, inc=1, device_id=(lower, dp), device_id_type=MESH)

    def weight_copy(layer, proj):
        copy = own if layer == 0 else 1 - own
        return pltpu.make_async_copy(wts.at[copy, proj], W.at[layer, proj], w_sem.at[layer, proj])

    for layer in range(2):
        for proj in range(2):
            weight_copy(layer, proj).start()

    token_copy = pltpu.make_async_copy(tok, ACT.at[0], t_sem.at[0])
    target_copy = pltpu.make_async_copy(tgt, TG, t_sem.at[1])

    @pl.when(stage == 0)
    def _():
        token_copy.start()
        target_copy.start()

    PS[NNZ] = jnp.zeros((R, BS), f32)

    pl.semaphore_wait(barrier, jnp.where((stage == 0) | (stage == STAGES - 1), 1, 2))

    for layer in range(2):
        for proj in range(2):
            weight_copy(layer, proj).wait()

    @pl.when(stage == 0)
    def _():
        token_copy.wait()
        target_copy.wait()

    def link(op, chunk, target):
        rows = pl.ds(pl.multiple_of(chunk * R, R), R)
        return pltpu.make_async_remote_copy(
            src_ref=OUT.at[op, :, rows, :],
            dst_ref=ACT.at[op, :, rows, :],
            send_sem=send_sem.at[op, chunk],
            recv_sem=recv_sem.at[op, chunk],
            device_id=(target, dp),
            device_id_type=MESH,
        )

    def chain(keep_base, lhs, block):
        def step(outer, acc):
            first = outer * UNROLL
            products = [
                jnp.dot(lhs(first + u), block(first + u), preferred_element_type=f32)
                for u in range(UNROLL)
            ]
            sums = []
            for u in range(UNROLL):
                acc = acc * keeps[keep_base + first + u] + products[u]
                sums.append(acc)
            for u in range(UNROLL):
                PS[first + u] = sums[u]
            return acc

        lax.fori_loop(0, NNZ // UNROLL, step, jnp.zeros((R, BS), f32))

    def transpose_weights():
        def step(outer, c):
            for layer in range(2):
                for proj in range(2):
                    turned = [W[layer, proj, outer * 8 + u].T for u in range(8)]
                    for u in range(8):
                        WT[layer, proj, outer * 8 + u] = turned[u]
            return c

        lax.fori_loop(0, NNZ // 8, step, 0)

    def item(i, carry):
        code = jnp.int32(0)
        for t in range(len(orders[0])):
            code = jnp.where(i == t, pick(stage, [o[t] for o in orders]), code)
        op, chunk = code // chunks, code % chunks
        layer = jnp.where((op == 1) | (op == 2), 1, 0)
        copy = jnp.where(layer == 0, own, 1 - own)
        base = copy * TABLE
        keep_base = copy * KEEPS
        rows = pl.ds(pl.multiple_of(chunk * R, R), R)
        even = op % 2 == 0
        source = jnp.where(even, lower, upper)
        target = jnp.where(even, upper, lower)
        first = jnp.where(even, stage == 0, stage == STAGES - 1)
        final = jnp.where(even, stage == STAGES - 1, stage == 0)

        @pl.when(i == jnp.where(stage < 2, chunks, 0))
        def _():
            transpose_weights()

        @pl.when(jnp.logical_not(first))
        def _():
            link(op, chunk, source).wait_recv()

        def factor_of(act_op):
            def square(b, acc):
                v = ACT[act_op, b, rows, :].astype(f32)
                return acc + v * v

            total = lax.fori_loop(0, DB, square, jnp.zeros((R, BS), f32), unroll=True)
            return lax.rsqrt(jnp.sum(total, axis=-1, keepdims=True) * (1.0 / D) + norm_eps)

        @pl.when(op < 2)
        def _():
            factor = factor_of(op)

            def normalize(b, c):
                v = ACT[op, b, rows, :].astype(f32)
                NORM[layer, b, rows, :] = (v * factor).astype(bf16)
                return c

            lax.fori_loop(0, DB, normalize, 0, unroll=True)
            chain(
                keep_base + K_UPF,
                lambda k: NORM[layer, tab[base + UPF_ROW + k], rows, :],
                lambda k: W[layer, 0, tab[base + UPF_PERM + k]],
            )

            def activate(outer, c):
                results = []
                for u in range(16):
                    a = PS[tab[base + UP_LAST + outer * 16 + u]]
                    sq = a * a
                    th = jnp.tanh(a * (gelu_coef + (gelu_coef * 0.044715) * sq))
                    half = 0.5 + 0.5 * th
                    slope = half + (0.5 * a) * (1.0 - th * th) * (
                        gelu_coef + (gelu_coef * 3.0 * 0.044715) * sq
                    )
                    results.append(((a * half).astype(bf16), slope.astype(bf16)))
                for u in range(16):
                    H[layer, outer * 16 + u, rows, :] = results[u][0]
                    S[layer, outer * 16 + u, rows, :] = results[u][1]
                return c

            lax.fori_loop(0, FB // 16, activate, 0)
            chain(
                keep_base + K_DNF,
                lambda k: H[layer, tab[base + DNF_ROW + k], rows, :],
                lambda k: W[layer, 1, tab[base + DNF_PERM + k]],
            )

            def mixed(b):
                v = ACT[op, b, rows, :].astype(f32)
                return (v + PS[tab[base + DN_LAST + b]]).astype(bf16)

            @pl.when(jnp.logical_not(final))
            def _():
                def put(b, c):
                    OUT[op, b, rows, :] = mixed(b)
                    return c

                lax.fori_loop(0, DB, put, 0, unroll=True)

            @pl.when(jnp.logical_and(final, op == 0))
            def _():
                def put(b, c):
                    ACT[1, b, rows, :] = mixed(b)
                    return c

                lax.fori_loop(0, DB, put, 0, unroll=True)

            @pl.when(jnp.logical_and(final, op == 1))
            def _():
                def put(b, c):
                    residue = mixed(b).astype(f32) - TG[b, rows, :].astype(f32)
                    ACT[2, b, rows, :] = residue.astype(bf16)
                    return c

                lax.fori_loop(0, DB, put, 0, unroll=True)

        @pl.when(op >= 2)
        def _():
            inputs = 3 - op
            for b in range(DB):
                COT[layer, b, rows, :] = ACT[op, b, rows, :]
            chain(
                keep_base + K_VB,
                lambda k: COT[layer, tab[base + VB_COL + k], rows, :],
                lambda k: WT[layer, 1, k],
            )

            def slope_times(outer, c):
                results = []
                for u in range(16):
                    g = PS[tab[base + VB_LAST + outer * 16 + u]]
                    results.append(g * S[layer, outer * 16 + u, rows, :].astype(f32))
                for u in range(16):
                    S[layer, outer * 16 + u, rows, :] = results[u].astype(bf16)
                return c

            lax.fori_loop(0, FB // 16, slope_times, 0)

            @pl.when(jnp.logical_not(jnp.logical_and(final, op == 3)))
            def _():
                chain(
                    keep_base + K_UB,
                    lambda k: S[layer, tab[base + UB_COL + k], rows, :],
                    lambda k: WT[layer, 0, k],
                )
                factor = factor_of(inputs)

                def couple(b, acc):
                    v = ACT[inputs, b, rows, :].astype(f32)
                    return acc + v * PS[tab[base + UB_LAST + b]]

                coupling = lax.fori_loop(0, DB, couple, jnp.zeros((R, BS), f32), unroll=True)
                coupling = jnp.sum(coupling, axis=-1, keepdims=True) * (1.0 / D)
                pull = factor * factor * factor * coupling

                def downstream(b):
                    v = ACT[inputs, b, rows, :].astype(f32)
                    g = PS[tab[base + UB_LAST + b]]
                    return (ACT[op, b, rows, :].astype(f32) + factor * g - v * pull).astype(bf16)

                @pl.when(jnp.logical_not(final))
                def _():
                    def put(b, c):
                        OUT[op, b, rows, :] = downstream(b)
                        return c

                    lax.fori_loop(0, DB, put, 0, unroll=True)

                @pl.when(final)
                def _():
                    def put(b, c):
                        ACT[3, b, rows, :] = downstream(b)
                        return c

                    lax.fori_loop(0, DB, put, 0, unroll=True)

        @pl.when(jnp.logical_not(final))
        def _():
            link(op, chunk, target).start()

        return carry

    lax.fori_loop(0, 4 * chunks, item, 0)

    def pair(lhs, rhs):
        return lax.dot_general(lhs, rhs, (((0,), (0,)), ((), ())), preferred_element_type=f32)

    def weight_gradients(layer):
        base = jnp.where(own == layer, 0, TABLE)
        for proj in range(2):

            def blocks(outer, c, proj=proj):
                parts = []
                for u in range(16):
                    k = outer * 16 + u
                    if proj == 0:
                        lhs = NORM[layer, tab[base + U_ROW + k]]
                        rhs = S[layer, tab[base + UB_COL + k]]
                    else:
                        lhs = H[layer, tab[base + V_ROW + k]]
                        rhs = COT[layer, tab[base + VB_COL + k]]
                    parts.append(pair(lhs, rhs))
                for v in range(8):
                    for d in range(16):
                        both = jnp.concatenate(
                            [p[8 * d : 8 * d + 8] for p in parts[2 * v : 2 * v + 2]], axis=0
                        )
                        place = d * 12 + proj * 6 + outer
                        W[layer, place // NNZ, place % NNZ, 16 * v : 16 * v + 16, :] = both.astype(bf16)
                return c

            lax.fori_loop(0, NNZ // 16, blocks, 0)

    weight_gradients(1)
    weight_gradients(0)
    for layer in range(2):
        for half in range(2):
            copy = own if layer == 0 else 1 - own
            pltpu.make_async_copy(W.at[layer, half], grads.at[copy, half], w_sem.at[layer, half]).start()
    for layer in range(2):
        for half in range(2):
            copy = own if layer == 0 else 1 - own
            pltpu.make_async_copy(W.at[layer, half], grads.at[copy, half], w_sem.at[layer, half]).wait()

    def drain(i, carry):
        op, chunk = i // chunks, i % chunks
        even = op % 2 == 0
        target = jnp.where(even, upper, lower)
        final = jnp.where(even, stage == STAGES - 1, stage == 0)

        @pl.when(jnp.logical_not(final))
        def _():
            link(op, chunk, target).wait_send()

        return carry

    lax.fori_loop(0, 4 * chunks, drain, 0)


def adam_update(grad_sum, master, moment, variance, token_total):
    gradient = grad_sum / token_total
    moment_next = beta_first * moment + (1.0 - beta_first) * gradient
    variance_next = beta_second * variance + (1.0 - beta_second) * gradient * gradient
    corrected = moment_next / (1.0 - beta_first**update_count)
    spread = jnp.sqrt(variance_next / (1.0 - beta_second**update_count))
    step_direction = corrected / (spread + adam_eps)
    return (step_direction, master - learn_rate * (step_direction + decay_rate * master))


def shards(tokens, targets, weights, pattern, master, moment, variance):
    section = lax.axis_index("section")
    dp_size = lax.axis_size("dp")
    row_count = tokens.shape[1] * tokens.shape[2]
    chunks = row_count // ROWS

    def stream_rows(values):
        mine = lax.dynamic_index_in_dim(values, section % 2, 0, keepdims=False)
        return mine.reshape(row_count, DB, BS).transpose(1, 0, 2)

    index, keeps = tables(pattern[0])
    orders = make_orders(chunks, 1.7, 2.3, 3.0)
    smem = pl.BlockSpec(memory_space=pltpu.SMEM)
    anywhere = pl.BlockSpec(memory_space=pl.ANY)
    grads = pl.pallas_call(
        functools.partial(pipeline_kernel, chunks, orders),
        out_shape=jax.ShapeDtypeStruct((2, 2, NNZ, BS, BS), bf16),
        in_specs=[smem, smem, anywhere, anywhere, anywhere],
        out_specs=anywhere,
        scratch_shapes=[
            pltpu.VMEM((2, 2, NNZ, BS, BS), bf16),
            pltpu.VMEM((2, 2, NNZ, BS, BS), bf16),
            pltpu.VMEM((4, DB, row_count, BS), bf16),
            pltpu.VMEM((4, DB, row_count, BS), bf16),
            pltpu.VMEM((2, DB, row_count, BS), bf16),
            pltpu.VMEM((2, DB, row_count, BS), bf16),
            pltpu.VMEM((2, FB, row_count, BS), bf16),
            pltpu.VMEM((2, FB, row_count, BS), bf16),
            pltpu.VMEM((DB, row_count, BS), bf16),
            pltpu.VMEM((NNZ + 1, ROWS, BS), f32),
            pltpu.SemaphoreType.DMA((2, 2)),
            pltpu.SemaphoreType.DMA((2,)),
            pltpu.SemaphoreType.DMA((4, chunks)),
            pltpu.SemaphoreType.DMA((4, chunks)),
        ],
        compiler_params=pltpu.CompilerParams(
            collective_id=0, has_side_effects=True, vmem_limit_bytes=58 * 1024 * 1024
        ),
    )(index, keeps, stream_rows(tokens), stream_rows(targets), weights[0])

    grads = grads.reshape(2, 16, 2 * NNZ * 8, BS)
    shares = lax.psum_scatter(grads, "dp", scatter_dimension=1, tiled=True)
    shares = shares.reshape(2, 16 // dp_size, 2, NNZ, 8, BS).transpose(0, 2, 3, 1, 4, 5)
    shares = shares.reshape((2,) + master.shape[1:])
    sections = lax.axis_size("section")
    arrived = lax.ppermute(shares[1], "section", [(s, sections - 1 - s) for s in range(sections)])
    token_total = 2 * row_count * dp_size
    step_direction, master_next = adam_update(
        shares[0].astype(f32) + arrived.astype(f32), master[0], moment[0], variance[0], token_total
    )
    return (step_direction[None], master_next[None])


def solution(mesh):
    return jax.shard_map(
        shards,
        mesh=mesh,
        in_specs=(
            P(None, None, "dp", None),
            P(None, None, "dp", None),
            P("section", None, None, None, None, None),
            P("section", None, None, None, None),
            P("section", None, None, "dp", None),
            P("section", None, None, "dp", None),
            P("section", None, None, "dp", None),
        ),
        out_specs=(P("section", None, None, "dp", None), P("section", None, None, "dp", None)),
        check_vma=False,
    )
```

time: 2440 us -> 485 us (0.20); the launches traced: 2400 us -> 481 us
  other arithmetic: 761 us -> 3.3 us
  starting transfers between devices: 524 us -> 4.22 us
  local copies, waits for them, and re-layouts: 501 us -> 9.56 us
  matrix products: 198 us -> 0 us
  Pallas kernels: 0 us -> 166 us
  waiting for transfers between devices: 357 us -> 284 us
  loops' own time: 46.1 us -> 0 us
    ppermute x47 -> x1, starting transfers between devices: 524 us -> 4.18 us  [shards(): lax.ppermute(shares[1], 'section', [(s, sections - 1 - s) for s in range(...]
    scatter-add x32 -> x0, other arithmetic: 320 us -> none  [the longest x16 160 us: sparse_transposed(): summed = jax.ops.segment_sum(product, put_index, num_segments=out_blocks)]
    scatter x143 -> x0, other arithmetic: 309 us -> none  [keep_slot(): return store.at[stream, slot_index].set(jnp.where(active, value, previous))]
    ppermute x47 -> x1, waiting for transfers between devices: 222 us -> 9.28 us  [shards(): lax.ppermute(shares[1], 'section', [(s, sections - 1 - s) for s in range(...]
    dot_general x36 -> x0, matrix products: 198 us -> none  [the longest x16 95.4 us: sparse_transposed(): jnp.einsum('rkb,kab->kra', picked, blocks, preferred_element_type=jnp.flo...]
    pallas_call x0 -> x1, Pallas kernels: none -> 166 us  [shards(): pl.pallas_call(functools.partial(pipeline_kernel, chunks, orders), out_sh...]
    dynamic_slice x176 -> x1, local copies, waits for them, and re-layouts: 167 us -> 1.58 us  [stream_rows(): mine = lax.dynamic_index_in_dim(values, section % 2, 0, keepdims=False)]
    unnamed x2, waiting for transfers between devices: 135 us -> 275 us
  transfers between devices with their start and end apart: 48 -> 2, of which waited for: 15 -> 2; matrix products, arithmetic and copies ran while one was open for 30% -> 0% of each run, Pallas kernels for 0% -> 0%
where the time goes in v1:
time: 485 us; the launch traced here: 481 us
  waiting for transfers between devices  284 us (59%)
  Pallas kernels  166 us (34%)
  between operations  14.2 us (3%)
  local copies, waits for them, and re-layouts  9.56 us (2%)
    unnamed x2, waiting for transfers between devices  275 us
    pallas_call x1, Pallas kernels, shards(): pl.pallas_call(functools.partial(pipeline_kernel, chunks, orders), out_sh...  166 us
  transfers between devices with their start and end apart: 2, of which 2 were waited for; matrix products, arithmetic and copies ran while one was open for 0% of the time, Pallas kernels for 0%

profile of v1, /device:TPU:0, one launch (start us, length us, event | category | flops | bytes accessed | tf_op | source)
XLA Modules:
  0.0 481.3 jit_solution(8987007736762476259)
XLA Ops:
  7.2 0.0 all-reduce.3.cloned.1.call-start
  7.2 0.7 copy.62
  7.9 0.1 convert_reduce_fusion.5
  8.1 0.1 compare_convert_fusion
  8.2 0.2 convert_reduce_fusion.1
  8.3 0.1 compare_convert_fusion.1
  8.4 1.6 constant_dynamic-slice_fusion.2
  10.0 0.2 copy.55
  10.2 1.2 copy.60
  11.3 0.2 copy.54
  11.5 1.2 copy.61
  12.8 0.1 convert_reduce_fusion.7
  12.9 0.2 convert_reduce_fusion.3
  13.1 0.2 convert_reduce_fusion
  13.3 0.3 select_reduce_fusion
  13.7 0.1 concatenate.6
  13.8 0.7 reshape.44.tab
  14.5 0.1 compare_convert_fusion.2
  14.5 0.1 compare_convert_fusion.3
  14.6 0.1 concatenate.7
  14.7 0.6 reshape.45.keeps
  15.3 166.0 %shard_map.86 = bf16[2,2,96,128,128]{4,3,2,1,0:T(8,128)(2,1)} custom-call(s32[1856]{0:T(1024)} %reshape.44.tab, f32[768]{0:T(1024)} %reshape.45.keeps, bf16[16,224,128]{2,1,0:T(8,128)(2,1)} %bitcast.104, bf16[16,224,128]{2,1,0:T(8,128)(2,1)} %bitcast.103, bf16[2,2,96,128,128]{4,3,2,1,0:T(8,128)(2,1)} %bitcast.98), custom_call_target="tpu_custom_call" | custom-call | tf_op jit(solution)/shard_map/pallas_call | solution.py:477
  181.3 0.0 copy-start.3
  181.3 0.0 copy-start
  181.3 0.0 copy-start.1
  181.4 0.0 copy-start.2
  181.4 0.0 all-reduce.3.cloned.1.call-update
  181.4 0.6 copy-done.3
  182.0 0.6 dynamic-slice
  182.6 274.8 %all-reduce.3.cloned.1.call-done = bf16[2,16,1536,128]{3,2,1,0:T(8,128)(2,1)} async-done(((bf16[2,16,1536,128]{3,2,1,0:T(8,128)(2,1)}), bf16[2,16,1536,128]{3,2,1,0:T(8,128)(2,1)}) %all-reduce.3.cloned.1.call-update) | async-done | bytes 12582928
  457.3 1.8 constant_dynamic-slice_fusion
  459.1 4.2 collective-permute-start
  463.3 9.3 %collective-permute-done = bf16[2,96,8,128]{3,2,1,0:T(8,128)(2,1)S(1)} collective-permute-done((bf16[2,96,8,128]{3,2,1,0:T(8,128)(2,1)S(1)}, bf16[2,96,8,128]{3,2,1,0:T(8,128)(2,1)S(1)}, u32[]{:S(2)}, u32[]{:S(2)}) %collective-permute-start) | collective-permute-done | bytes 393248 | tf_op jit(solution)/shard_map/ppermute | solution.py:508
  472.6 0.0 copy-done
  472.6 0.0 copy-done.1
  472.6 0.0 copy-done.2
  472.6 1.8 fusion.2
  (14 shorter events, 0.1 us)
Async XLA Ops:
  7.2 450.2 %all-reduce.3.cloned.1.call-start = ((), (), s32[]{:S(2)}) async-start(), calls=%async_computation | async-start | bytes 25165824
  181.3 0.7 copy-start.3
  181.3 291.3 %copy-start = (f32[1,2,96,8,128]{4,3,2,1,0:T(8,128)S(1)}, f32[1,2,96,8,128]{4,3,2,1,0:T(8,128)}, u32[]{:S(2)}) copy-start(f32[1,2,96,8,128]{4,3,2,1,0:T(8,128)} %param.11) | copy-start | bytes 2359300
  181.3 291.3 %copy-start.1 = (f32[1,2,96,8,128]{4,3,2,1,0:T(8,128)S(1)}, f32[1,2,96,8,128]{4,3,2,1,0:T(8,128)}, u32[]{:S(2)}) copy-start(f32[1,2,96,8,128]{4,3,2,1,0:T(8,128)} %param.13) | copy-start | bytes 2359300
  181.4 291.2 %copy-start.2 = (f32[1,2,96,8,128]{4,3,2,1,0:T(8,128)S(1)}, f32[1,2,96,8,128]{4,3,2,1,0:T(8,128)}, u32[]{:S(2)}) copy-start(f32[1,2,96,8,128]{4,3,2,1,0:T(8,128)} %param.12) | copy-start | bytes 2359300
  459.1 13.5 %collective-permute-start = (bf16[2,96,8,128]{3,2,1,0:T(8,128)(2,1)S(1)}, bf16[2,96,8,128]{3,2,1,0:T(8,128)(2,1)S(1)}, u32[]{:S(2)}, u32[]{:S(2)}) collective-permute-start(bf16[2,96,8,128]{3,2,1,0:T(8,128)(2,1)S(1)} %bitcast.107), channel_id=1, source_target_pairs={{0,112},{16,96},{32,80},{48,64},{64,48},{80,32},{96,16},{112,0},{1... | collective-permute-start | bytes 1179656 | tf_op jit(solution)/shard_map/ppermute | solution.py:508
Sparse Core Ops, SparseCore 0:
  181.5 275.7 all-reduce.2

commit v2 on v1

--- a/solution.py
+++ b/solution.py
@@ -16,6 +16,8 @@
 STAGES = 4
 ROWS = 32
 UNROLL = 48
+STEPS = 6
+SLICE = 6
 
 norm_eps = 1e-06
 gelu_coef = 0.7978845608028654
@@ -58,6 +60,36 @@
         elif op < 3:
             arrival[(stage, op + 1, chunk)] = end
     return orders
+
+
+def make_sequences(chunks, orders):
+    items = 4 * chunks
+    sequences = []
+    for order in orders:
+        turn = order.index(2 * chunks + chunks - 1)
+        code = lambda step, role: items + 2 * step + role
+        first = [(turn, 0)] + [(turn + gap, step) for step, gap in ((1, 2), (2, 4), (3, 7))]
+        placed = {}
+        for at, step in first:
+            if at < items and turn < items - 2:
+                placed.setdefault(at, []).append(code(step, 1))
+        sequence = []
+        for n, item in enumerate(order):
+            sequence.append(item)
+            sequence.extend(placed.get(n, []))
+        done = sum(len(v) for v in placed.values())
+        early = [code(step, 1) for step in range(done, STEPS)]
+        late = [code(step, 0) for step in range(STEPS)]
+        if done == 0:
+            sequence.append(early.pop(0))
+        sequence.append(late.pop(0))
+        while early or late:
+            if early:
+                sequence.append(early.pop(0))
+            if late:
+                sequence.append(late.pop(0))
+        sequences.append(sequence)
+    return sequences
 
 
 def tables(pattern):
@@ -113,13 +145,13 @@
 
 def pipeline_kernel(
     chunks,
-    orders,
+    sequences,
     tab,
     keeps,
     tok,
     tgt,
     wts,
-    grads,
+    sums_out,
     W,
     WT,
     ACT,
@@ -134,6 +166,9 @@
     t_sem,
     send_sem,
     recv_sem,
+    share_send,
+    share_recv,
+    ready_sem,
 ):
     R = ROWS
     total_rows = chunks * R
@@ -149,6 +184,15 @@
     upper = section_of(stage + 1)
     lower = section_of(stage - 1)
 
+    core, z_lo, y = dp % 2, (dp // 2) % 2, dp // 4
+    y_up, y_down, y_far = (y + 1) % 4, (y + 3) % 4, (y + 2) % 4
+    peer_core = (section, dp + 1 - 2 * core)
+    peer_up = (section, y_up * 4 + z_lo * 2 + core)
+    peer_down = (section, y_down * 4 + z_lo * 2 + core)
+    peer_z = (section, dp + 2 - 4 * z_lo)
+    mirror = (7 - section, dp)
+    peers = (peer_core, peer_up, peer_down, peer_z, mirror)
+
     barrier = pltpu.get_barrier_semaphore()
 
     @pl.when(stage < STAGES - 1)
@@ -158,6 +202,9 @@
     @pl.when(stage > 0)
     def _():
         pl.semaphore_signal(barrier, inc=1, device_id=(lower, dp), device_id_type=MESH)
+
+    for peer in peers:
+        pl.semaphore_signal(barrier, inc=1, device_id=peer, device_id_type=MESH)
 
     def weight_copy(layer, proj):
         copy = own if layer == 0 else 1 - own
@@ -177,7 +224,7 @@
 
     PS[NNZ] = jnp.zeros((R, BS), f32)
 
-    pl.semaphore_wait(barrier, jnp.where((stage == 0) | (stage == STAGES - 1), 1, 2))
+    pl.semaphore_wait(barrier, jnp.where((stage == 0) | (stage == STAGES - 1), 6, 7))
 
     for layer in range(2):
         for proj in range(2):
@@ -227,10 +274,7 @@
 
         lax.fori_loop(0, NNZ // 8, step, 0)
 
-    def item(i, carry):
-        code = jnp.int32(0)
-        for t in range(len(orders[0])):
-            code = jnp.where(i == t, pick(stage, [o[t] for o in orders]), code)
+    def item(code):
         op, chunk = code // chunks, code % chunks
         layer = jnp.where((op == 1) | (op == 2), 1, 0)
         copy = jnp.where(layer == 0, own, 1 - own)
@@ -242,10 +286,6 @@
         target = jnp.where(even, upper, lower)
         first = jnp.where(even, stage == 0, stage == STAGES - 1)
         final = jnp.where(even, stage == STAGES - 1, stage == 0)
-
-        @pl.when(i == jnp.where(stage < 2, chunks, 0))
-        def _():
-            transpose_weights()
 
         @pl.when(jnp.logical_not(first))
         def _():
@@ -391,49 +431,168 @@
         def _():
             link(op, chunk, target).start()
 
-        return carry
-
-    lax.fori_loop(0, 4 * chunks, item, 0)
-
     def pair(lhs, rhs):
         return lax.dot_general(lhs, rhs, (((0,), (0,)), ((), ())), preferred_element_type=f32)
 
-    def weight_gradients(layer):
-        base = jnp.where(own == layer, 0, TABLE)
-        for proj in range(2):
-
-            def blocks(outer, c, proj=proj):
-                parts = []
-                for u in range(16):
-                    k = outer * 16 + u
+    def weight_gradient(role, proj):
+        base = jnp.where(role == 0, own, 1 - own) * TABLE
+
+        def blocks(outer, c):
+            parts = []
+            for u in range(16):
+                k = outer * 16 + u
+                if proj == 0:
+                    lhs = NORM[role, tab[base + U_ROW + k]]
+                    rhs = S[role, tab[base + UB_COL + k]]
+                else:
+                    lhs = H[role, tab[base + V_ROW + k]]
+                    rhs = COT[role, tab[base + VB_COL + k]]
+                parts.append(pair(lhs, rhs))
+            for v in range(8):
+                for d in range(16):
+                    both = jnp.concatenate(
+                        [p[8 * d : 8 * d + 8] for p in parts[2 * v : 2 * v + 2]], axis=0
+                    )
+                    place = (d % 2) * 8 + (d // 4) * 2 + (d // 2) % 2
+                    W[role, proj, place * SLICE + outer, 16 * v : 16 * v + 16, :] = both.astype(bf16)
+            return c
+
+        lax.fori_loop(0, NNZ // 16, blocks, 0)
+
+    mine = core * 8 * SLICE
+
+    def unit(of_y, of_z=0):
+        return mine + (of_y * 2 + of_z) * SLICE
+
+    def share_copy(role, proj, number):
+        source, landing, count, peer = (
+            ((1 - core) * 8 * SLICE, 0, 8 * SLICE, peer_core),
+            (unit(y_far, 0), 48, SLICE, peer_up),
+            (unit(y_far, 1), 54, SLICE, peer_down),
+            (unit(y_up), 60, 2 * SLICE, peer_up),
+            (unit(y_down), 72, 2 * SLICE, peer_down),
+            (unit(y, 1 - z_lo), 84, SLICE, peer_z),
+            (unit(y, z_lo), 90, SLICE, mirror),
+        )[number]
+        return pltpu.make_async_remote_copy(
+            src_ref=W.at[role, proj, pl.ds(source, count)],
+            dst_ref=WT.at[role, proj, pl.ds(landing, count)],
+            send_sem=share_send.at[role, proj, number],
+            recv_sem=share_recv.at[role, proj, number],
+            device_id=peer,
+            device_id_type=MESH,
+        )
+
+    def add(role, proj, place, landing, count):
+        def step(n, c):
+            there = WT[role, proj, landing + n].astype(f32)
+            W[role, proj, place + n] = (W[role, proj, place + n].astype(f32) + there).astype(bf16)
+            return c
+
+        lax.fori_loop(0, count, step, 0, unroll=2)
+
+    def add_two(role, proj, place, landing, other, count):
+        def step(n, c):
+            there = WT[role, proj, landing + n].astype(f32) + WT[role, proj, other + n].astype(f32)
+            W[role, proj, place + n] = (W[role, proj, place + n].astype(f32) + there).astype(bf16)
+            return c
+
+        lax.fori_loop(0, count, step, 0, unroll=2)
+
+    def action(code):
+        step, role = (code - 4 * chunks) // 2, (code - 4 * chunks) % 2
+        owner = own == role
+
+        @pl.when(step == 0)
+        def _():
+            for number, peer in enumerate(peers[:4]):
+                pl.semaphore_signal(ready_sem.at[role, number], inc=1, device_id=peer, device_id_type=MESH)
+
+            @pl.when(owner)
+            def _():
+                pl.semaphore_signal(ready_sem.at[role, 4], inc=1, device_id=mirror, device_id_type=MESH)
+
+            weight_gradient(role, 0)
+            pl.semaphore_wait(ready_sem.at[role, 0], 1)
+            share_copy(role, 0, 0).start()
+            weight_gradient(role, 1)
+            share_copy(role, 1, 0).start()
+
+        @pl.when(step == 1)
+        def _():
+            for proj in range(2):
+                share_copy(role, proj, 0).wait_recv()
+                add(role, proj, mine, 0, 8 * SLICE)
+                if proj == 0:
+                    pl.semaphore_wait(ready_sem.at[role, 1], 1)
+                    pl.semaphore_wait(ready_sem.at[role, 2], 1)
+                share_copy(role, proj, 1).start()
+                share_copy(role, proj, 2).start()
+
+        @pl.when(step == 2)
+        def _():
+            for proj in range(2):
+                share_copy(role, proj, 1).wait_recv()
+                add(role, proj, unit(y_up, 0), 48, SLICE)
+                share_copy(role, proj, 3).start()
+                share_copy(role, proj, 2).wait_recv()
+                add(role, proj, unit(y_down, 1), 54, SLICE)
+                share_copy(role, proj, 4).start()
+
+        @pl.when(step == 3)
+        def _():
+            for proj in range(2):
+                share_copy(role, proj, 3).wait_recv()
+                share_copy(role, proj, 4).wait_recv()
+                add_two(role, proj, unit(y, 0), 60, 72, 2 * SLICE)
+                if proj == 0:
+                    pl.semaphore_wait(ready_sem.at[role, 3], 1)
+                share_copy(role, proj, 5).start()
+
+        @pl.when(step == 4)
+        def _():
+            for proj in range(2):
+                share_copy(role, proj, 5).wait_recv()
+                add(role, proj, unit(y, z_lo), 84, SLICE)
+
+                @pl.when(jnp.logical_not(owner))
+                def _(proj=proj):
                     if proj == 0:
-                        lhs = NORM[layer, tab[base + U_ROW + k]]
-                        rhs = S[layer, tab[base + UB_COL + k]]
-                    else:
-                        lhs = H[layer, tab[base + V_ROW + k]]
-                        rhs = COT[layer, tab[base + VB_COL + k]]
-                    parts.append(pair(lhs, rhs))
-                for v in range(8):
-                    for d in range(16):
-                        both = jnp.concatenate(
-                            [p[8 * d : 8 * d + 8] for p in parts[2 * v : 2 * v + 2]], axis=0
-                        )
-                        place = d * 12 + proj * 6 + outer
-                        W[layer, place // NNZ, place % NNZ, 16 * v : 16 * v + 16, :] = both.astype(bf16)
-                return c
-
-            lax.fori_loop(0, NNZ // 16, blocks, 0)
-
-    weight_gradients(1)
-    weight_gradients(0)
-    for layer in range(2):
-        for half in range(2):
-            copy = own if layer == 0 else 1 - own
-            pltpu.make_async_copy(W.at[layer, half], grads.at[copy, half], w_sem.at[layer, half]).start()
-    for layer in range(2):
-        for half in range(2):
-            copy = own if layer == 0 else 1 - own
-            pltpu.make_async_copy(W.at[layer, half], grads.at[copy, half], w_sem.at[layer, half]).wait()
+                        pl.semaphore_wait(ready_sem.at[role, 4], 1)
+                    share_copy(role, proj, 6).start()
+
+        @pl.when(jnp.logical_and(step == 5, owner))
+        def _():
+            for proj in range(2):
+                share_copy(role, proj, 6).wait_recv()
+
+                def total(n, c, proj=proj):
+                    there = WT[role, proj, 90 + n].astype(f32)
+                    sums_out[proj, n] = W[role, proj, unit(y, z_lo) + n].astype(f32) + there
+                    return c
+
+                lax.fori_loop(0, SLICE, total, 0)
+
+    def turn(i, carry):
+        code = jnp.int32(0)
+        for t in range(len(sequences[0])):
+            code = jnp.where(i == t, pick(stage, [o[t] for o in sequences]), code)
+
+        @pl.when(i == jnp.where(stage < 2, chunks, 0))
+        def _():
+            transpose_weights()
+
+        @pl.when(code < 4 * chunks)
+        def _():
+            item(code)
+
+        @pl.when(code >= 4 * chunks)
+        def _():
+            action(code)
+
+        return carry
+
+    lax.fori_loop(0, len(sequences[0]), turn, 0)
 
     def drain(i, carry):
         op, chunk = i // chunks, i % chunks
@@ -448,6 +607,14 @@
         return carry
 
     lax.fori_loop(0, 4 * chunks, drain, 0)
+    for role in range(2):
+        for proj in range(2):
+            for number in range(6):
+                share_copy(role, proj, number).wait_send()
+
+            @pl.when(own != role)
+            def _(role=role, proj=proj):
+                share_copy(role, proj, 6).wait_send()
 
 
 def adam_update(grad_sum, master, moment, variance, token_total):
@@ -475,10 +642,10 @@
     smem = pl.BlockSpec(memory_space=pltpu.SMEM)
     anywhere = pl.BlockSpec(memory_space=pl.ANY)
     grads = pl.pallas_call(
-        functools.partial(pipeline_kernel, chunks, orders),
-        out_shape=jax.ShapeDtypeStruct((2, 2, NNZ, BS, BS), bf16),
+        functools.partial(pipeline_kernel, chunks, make_sequences(chunks, orders)),
+        out_shape=jax.ShapeDtypeStruct((2, SLICE, BS, BS), f32),
         in_specs=[smem, smem, anywhere, anywhere, anywhere],
-        out_specs=anywhere,
+        out_specs=pl.BlockSpec(memory_space=pltpu.VMEM),
         scratch_shapes=[
             pltpu.VMEM((2, 2, NNZ, BS, BS), bf16),
             pltpu.VMEM((2, 2, NNZ, BS, BS), bf16),
@@ -494,21 +661,18 @@
             pltpu.SemaphoreType.DMA((2,)),
             pltpu.SemaphoreType.DMA((4, chunks)),
             pltpu.SemaphoreType.DMA((4, chunks)),
+            pltpu.SemaphoreType.DMA((2, 2, 7)),
+            pltpu.SemaphoreType.DMA((2, 2, 7)),
+            pltpu.SemaphoreType.REGULAR((2, 5)),
         ],
         compiler_params=pltpu.CompilerParams(
-            collective_id=0, has_side_effects=True, vmem_limit_bytes=58 * 1024 * 1024
+            collective_id=0, has_side_effects=True, vmem_limit_bytes=60 * 1024 * 1024
         ),
     )(index, keeps, stream_rows(tokens), stream_rows(targets), weights[0])
 
-    grads = grads.reshape(2, 16, 2 * NNZ * 8, BS)
-    shares = lax.psum_scatter(grads, "dp", scatter_dimension=1, tiled=True)
-    shares = shares.reshape(2, 16 // dp_size, 2, NNZ, 8, BS).transpose(0, 2, 3, 1, 4, 5)
-    shares = shares.reshape((2,) + master.shape[1:])
-    sections = lax.axis_size("section")
-    arrived = lax.ppermute(shares[1], "section", [(s, sections - 1 - s) for s in range(sections)])
     token_total = 2 * row_count * dp_size
     step_direction, master_next = adam_update(
-        shares[0].astype(f32) + arrived.astype(f32), master[0], moment[0], variance[0], token_total
+        grads.reshape(master.shape[1:]), master[0], moment[0], variance[0], token_total
     )
     return (step_direction[None], master_next[None])
 

time: 485 us -> 221 us (0.46)
  waiting for transfers between devices: 284 us -> 0 us
  Pallas kernels: 166 us -> 208 us
  between operations: 14.2 us -> 0.78 us
    unnamed x2 -> x0, waiting for transfers between devices: 275 us -> none
    pallas_call x1, Pallas kernels: 166 us -> 208 us  [shards(): pl.pallas_call(functools.partial(pipeline_kernel, chunks, make_sequences(...]
    ppermute x1 -> x0, waiting for transfers between devices: 9.28 us -> none  [shards(): lax.ppermute(shares[1], 'section', [(s, sections - 1 - s) for s in range(...]
  transfers between devices with their start and end apart: 2 -> 0, of which waited for: 2 -> 0; matrix products, arithmetic and copies ran while one was open for 0% -> 0% of each run, Pallas kernels for 0% -> 0%
where the time goes in v2:
time: 221 us; the launch traced here: 220 us
  Pallas kernels  208 us (94%)
  local copies, waits for them, and re-layouts  6.87 us (3%)
  other arithmetic  4.57 us (2%)
    pallas_call x1, Pallas kernels, shards(): pl.pallas_call(functools.partial(pipeline_kernel, chunks, make_sequences(...  208 us

profile of v2, /device:TPU:0, one launch (start us, length us, event | category | flops | bytes accessed | tf_op | source)
XLA Modules:
  0.0 220.3 jit_solution(10527348998635227628)
XLA Ops:
  0.6 0.7 copy.51
  1.4 0.2 convert_reduce_fusion
  1.6 0.3 select_reduce_fusion
  1.9 0.1 compare_convert_fusion.2
  2.0 0.1 compare_convert_fusion.3
  2.1 0.1 compare_convert_fusion
  2.2 0.1 compare_convert_fusion.1
  2.2 0.1 concatenate.7
  2.3 0.6 reshape.72.keeps
  2.9 0.1 convert_reduce_fusion.3
  3.1 0.1 convert_reduce_fusion.7
  3.3 0.1 convert_reduce_fusion.5
  3.4 0.1 convert_reduce_fusion.1
  3.6 0.1 concatenate.6
  3.7 0.7 reshape.71.tab
  4.4 1.6 constant_dynamic-slice_fusion
  6.0 0.2 copy.43
  6.1 1.2 copy.50
  7.3 0.2 copy.44
  7.5 1.2 copy.49
  8.7 208.1 %shard_map.86 = f32[2,6,128,128]{3,2,1,0:T(8,128)} custom-call(s32[1856]{0:T(1024)} %reshape.71.tab, f32[768]{0:T(1024)} %reshape.72.keeps, bf16[16,224,128]{2,1,0:T(8,128)(2,1)} %bitcast.61, bf16[16,224,128]{2,1,0:T(8,128)(2,1)} %bitcast.62, bf16[2,2,96,128,128]{4,3,2,1,0:T(8,128)(2,1)} %bitcast.56), custom_call_target="tpu_custom_call" | custom-call | tf_op jit(solution)/shard_map/pallas_call | solution.py:644
  216.8 0.0 copy-start
  216.8 0.0 copy-start.1
  216.8 0.0 copy-start.2
  216.8 1.5 broadcast_multiply_fusion
  218.3 0.0 copy-done
  218.3 0.1 copy-done.1
  218.4 0.2 copy-done.2
  218.6 1.7 multiply_subtract_fusion
  (14 shorter events, 0.1 us)
Async XLA Ops:
  216.8 1.5 copy-start
  216.8 1.6 copy-start.1
  216.8 1.8 copy-start.2

commit v3 on v2

--- a/solution.py
+++ b/solution.py
@@ -15,8 +15,7 @@
 FB = FF // BS
 STAGES = 4
 ROWS = 32
-UNROLL = 48
-STEPS = 6
+STEPS = 7
 SLICE = 6
 
 norm_eps = 1e-06
@@ -71,7 +70,7 @@
         first = [(turn, 0)] + [(turn + gap, step) for step, gap in ((1, 2), (2, 4), (3, 7))]
         placed = {}
         for at, step in first:
-            if at < items and turn < items - 2:
+            if at < items - 1 and turn < items - 2:
                 placed.setdefault(at, []).append(code(step, 1))
         sequence = []
         for n, item in enumerate(order):
@@ -174,17 +173,16 @@
     total_rows = chunks * R
     section = lax.axis_index("section")
     dp = lax.axis_index("dp")
-    x, z_hi = section // 2, section % 2
+    z_hi = section % 2
     stage = jnp.where(section < 4, section, 7 - section)
     own = jnp.where(section < 4, 0, 1)
 
+    core, z_lo, y = dp % 2, (dp // 2) % 2, dp // 4
     def section_of(s):
         return jnp.where(s % 2 == z_hi, s, 7 - s)
 
-    upper = section_of(stage + 1)
-    lower = section_of(stage - 1)
-
-    core, z_lo, y = dp % 2, (dp // 2) % 2, dp // 4
+    upper = section_of(jnp.minimum(stage + 1, STAGES - 1))
+    lower = section_of(jnp.maximum(stage - 1, 0))
     y_up, y_down, y_far = (y + 1) % 4, (y + 3) % 4, (y + 2) % 4
     peer_core = (section, dp + 1 - 2 * core)
     peer_up = (section, y_up * 4 + z_lo * 2 + core)
@@ -214,13 +212,18 @@
         for proj in range(2):
             weight_copy(layer, proj).start()
 
-    token_copy = pltpu.make_async_copy(tok, ACT.at[0], t_sem.at[0])
-    target_copy = pltpu.make_async_copy(tgt, TG, t_sem.at[1])
+    def row_copies():
+        for b in range(DB):
+            columns = pl.ds(b * BS, BS)
+            yield pltpu.make_async_copy(tok.at[z_hi, :, columns], ACT.at[0, b], t_sem.at[0, b])
+        for b in range(DB):
+            columns = pl.ds(b * BS, BS)
+            yield pltpu.make_async_copy(tgt.at[z_hi, :, columns], TG.at[b], t_sem.at[1, b])
 
     @pl.when(stage == 0)
     def _():
-        token_copy.start()
-        target_copy.start()
+        for copy in row_copies():
+            copy.start()
 
     PS[NNZ] = jnp.zeros((R, BS), f32)
 
@@ -232,8 +235,8 @@
 
     @pl.when(stage == 0)
     def _():
-        token_copy.wait()
-        target_copy.wait()
+        for copy in row_copies():
+            copy.wait()
 
     def link(op, chunk, target):
         rows = pl.ds(pl.multiple_of(chunk * R, R), R)
@@ -246,22 +249,28 @@
             device_id_type=MESH,
         )
 
-    def chain(keep_base, lhs, block):
-        def step(outer, acc):
-            first = outer * UNROLL
-            products = [
-                jnp.dot(lhs(first + u), block(first + u), preferred_element_type=f32)
-                for u in range(UNROLL)
-            ]
+    def chain(keep_base, lhs, block, group=16, then=None):
+        acc = jnp.zeros((R, BS), f32)
+        done = 0
+        for first in range(0, NNZ, group):
+            slots = range(first, first + group)
+            products = [jnp.dot(lhs(k), block(k), preferred_element_type=f32) for k in slots]
+            stores = []
+            if then is not None:
+                ended = max(0, first - (NNZ - FB))
+                stores = [then(j) for j in range(done, ended)]
+                done = ended
             sums = []
-            for u in range(UNROLL):
+            for u in range(group):
                 acc = acc * keeps[keep_base + first + u] + products[u]
                 sums.append(acc)
-            for u in range(UNROLL):
+            for u in range(group):
                 PS[first + u] = sums[u]
-            return acc
-
-        lax.fori_loop(0, NNZ // UNROLL, step, jnp.zeros((R, BS), f32))
+            for store in stores:
+                store()
+        if then is not None:
+            for store in [then(j) for j in range(done, FB)]:
+                store()
 
     def transpose_weights():
         def step(outer, c):
@@ -309,29 +318,30 @@
                 return c
 
             lax.fori_loop(0, DB, normalize, 0, unroll=True)
+            def activate(j):
+                a = PS[tab[base + UP_LAST + j]]
+                sq = a * a
+                th = jnp.tanh(a * (gelu_coef + (gelu_coef * 0.044715) * sq))
+                half = 0.5 + 0.5 * th
+                slope = half + (0.5 * a) * (1.0 - th * th) * (
+                    gelu_coef + (gelu_coef * 3.0 * 0.044715) * sq
+                )
+                hidden = (a * half).astype(bf16)
+                slope = slope.astype(bf16)
+
+                def store():
+                    H[layer, j, rows, :] = hidden
+                    S[layer, j, rows, :] = slope
+
+                return store
+
             chain(
                 keep_base + K_UPF,
                 lambda k: NORM[layer, tab[base + UPF_ROW + k], rows, :],
                 lambda k: W[layer, 0, tab[base + UPF_PERM + k]],
+                group=8,
+                then=activate,
             )
-
-            def activate(outer, c):
-                results = []
-                for u in range(16):
-                    a = PS[tab[base + UP_LAST + outer * 16 + u]]
-                    sq = a * a
-                    th = jnp.tanh(a * (gelu_coef + (gelu_coef * 0.044715) * sq))
-                    half = 0.5 + 0.5 * th
-                    slope = half + (0.5 * a) * (1.0 - th * th) * (
-                        gelu_coef + (gelu_coef * 3.0 * 0.044715) * sq
-                    )
-                    results.append(((a * half).astype(bf16), slope.astype(bf16)))
-                for u in range(16):
-                    H[layer, outer * 16 + u, rows, :] = results[u][0]
-                    S[layer, outer * 16 + u, rows, :] = results[u][1]
-                return c
-
-            lax.fori_loop(0, FB // 16, activate, 0)
             chain(
                 keep_base + K_DNF,
                 lambda k: H[layer, tab[base + DNF_ROW + k], rows, :],
@@ -372,22 +382,21 @@
             inputs = 3 - op
             for b in range(DB):
                 COT[layer, b, rows, :] = ACT[op, b, rows, :]
+            def slope_times(j):
+                g = PS[tab[base + VB_LAST + j]]
+                result = (g * S[layer, j, rows, :].astype(f32)).astype(bf16)
+
+                def store():
+                    S[layer, j, rows, :] = result
+
+                return store
+
             chain(
                 keep_base + K_VB,
                 lambda k: COT[layer, tab[base + VB_COL + k], rows, :],
                 lambda k: WT[layer, 1, k],
+                then=slope_times,
             )
-
-            def slope_times(outer, c):
-                results = []
-                for u in range(16):
-                    g = PS[tab[base + VB_LAST + outer * 16 + u]]
-                    results.append(g * S[layer, outer * 16 + u, rows, :].astype(f32))
-                for u in range(16):
-                    S[layer, outer * 16 + u, rows, :] = results[u].astype(bf16)
-                return c
-
-            lax.fori_loop(0, FB // 16, slope_times, 0)
 
             @pl.when(jnp.logical_not(jnp.logical_and(final, op == 3)))
             def _():
@@ -453,27 +462,43 @@
                     both = jnp.concatenate(
                         [p[8 * d : 8 * d + 8] for p in parts[2 * v : 2 * v + 2]], axis=0
                     )
-                    place = (d % 2) * 8 + (d // 4) * 2 + (d // 2) % 2
+                    of_core, of_y, of_z = d % 2, d // 4, (d // 2) % 2
+                    place = of_core * 8 + (of_y * 2 + of_z if proj == 0 else of_z * 4 + of_y)
                     W[role, proj, place * SLICE + outer, 16 * v : 16 * v + 16, :] = both.astype(bf16)
             return c
 
-        lax.fori_loop(0, NNZ // 16, blocks, 0)
+        lax.fori_loop(0, SLICE, blocks, 0)
 
     mine = core * 8 * SLICE
 
-    def unit(of_y, of_z=0):
-        return mine + (of_y * 2 + of_z) * SLICE
+    def unit(proj, of_y, of_z):
+        return mine + (of_y * 2 + of_z if proj == 0 else of_z * 4 + of_y) * SLICE
+
+    CORE, FAR_UP, FAR_DOWN, UP, DOWN, Z, MIRROR = range(7)
+    half = SLICE // 2
+    copies = (
+        (
+            ((1 - core) * 8 * SLICE, 0, 48, peer_core),
+            (unit(0, y_far, 0), 48, SLICE, peer_up),
+            (unit(0, y_far, 1), 54, SLICE, peer_down),
+            (unit(0, y_up, 0), 60, 2 * SLICE, peer_up),
+            (unit(0, y_down, 0), 72, 2 * SLICE, peer_down),
+            (unit(0, y, 1 - z_lo), 84, SLICE, peer_z),
+            (unit(0, y, z_lo), 90, SLICE, mirror),
+        ),
+        (
+            ((1 - core) * 8 * SLICE, 0, 48, peer_core),
+            (unit(1, y_far, z_lo), 48, half, peer_up),
+            (unit(1, y_far, z_lo) + half, 51, half, peer_down),
+            (unit(1, y_up, z_lo), 54, SLICE, peer_up),
+            (unit(1, y_down, z_lo), 60, SLICE, peer_down),
+            (unit(1, 0, 1 - z_lo), 66, 4 * SLICE, peer_z),
+            (unit(1, y, z_lo), 90, SLICE, mirror),
+        ),
+    )
 
     def share_copy(role, proj, number):
-        source, landing, count, peer = (
-            ((1 - core) * 8 * SLICE, 0, 8 * SLICE, peer_core),
-            (unit(y_far, 0), 48, SLICE, peer_up),
-            (unit(y_far, 1), 54, SLICE, peer_down),
-            (unit(y_up), 60, 2 * SLICE, peer_up),
-            (unit(y_down), 72, 2 * SLICE, peer_down),
-            (unit(y, 1 - z_lo), 84, SLICE, peer_z),
-            (unit(y, z_lo), 90, SLICE, mirror),
-        )[number]
+        source, landing, count, peer = copies[proj][number]
         return pltpu.make_async_remote_copy(
             src_ref=W.at[role, proj, pl.ds(source, count)],
             dst_ref=WT.at[role, proj, pl.ds(landing, count)],
@@ -483,26 +508,37 @@
             device_id_type=MESH,
         )
 
-    def add(role, proj, place, landing, count):
+    def add(role, proj, place, *numbers):
+        for number in numbers:
+            share_copy(role, proj, number).wait_recv()
+
         def step(n, c):
-            there = WT[role, proj, landing + n].astype(f32)
-            W[role, proj, place + n] = (W[role, proj, place + n].astype(f32) + there).astype(bf16)
+            total = W[role, proj, place + n].astype(f32)
+            for number in numbers:
+                total = total + WT[role, proj, copies[proj][number][1] + n].astype(f32)
+            W[role, proj, place + n] = total.astype(bf16)
             return c
 
-        lax.fori_loop(0, count, step, 0, unroll=2)
-
-    def add_two(role, proj, place, landing, other, count):
-        def step(n, c):
-            there = WT[role, proj, landing + n].astype(f32) + WT[role, proj, other + n].astype(f32)
-            W[role, proj, place + n] = (W[role, proj, place + n].astype(f32) + there).astype(bf16)
-            return c
-
-        lax.fori_loop(0, count, step, 0, unroll=2)
+        lax.fori_loop(0, copies[proj][numbers[0]][2], step, 0, unroll=3)
+
+    def send(role, proj, *numbers):
+        for number in numbers:
+            share_copy(role, proj, number).start()
 
     def action(code):
         step, role = (code - 4 * chunks) // 2, (code - 4 * chunks) % 2
         owner = own == role
 
+        def wait_ready(number):
+            pl.semaphore_wait(ready_sem.at[role, number], 1)
+
+        def send_mirror(proj):
+            @pl.when(jnp.logical_not(owner))
+            def _():
+                if proj == 0:
+                    wait_ready(4)
+                send(role, proj, MIRROR)
+
         @pl.when(step == 0)
         def _():
             for number, peer in enumerate(peers[:4]):
@@ -512,66 +548,57 @@
             def _():
                 pl.semaphore_signal(ready_sem.at[role, 4], inc=1, device_id=mirror, device_id_type=MESH)
 
+            weight_gradient(role, 1)
+            wait_ready(0)
+            send(role, 1, CORE)
             weight_gradient(role, 0)
-            pl.semaphore_wait(ready_sem.at[role, 0], 1)
-            share_copy(role, 0, 0).start()
-            weight_gradient(role, 1)
-            share_copy(role, 1, 0).start()
+            send(role, 0, CORE)
 
         @pl.when(step == 1)
         def _():
+            add(role, 1, mine, CORE)
+            wait_ready(3)
+            send(role, 1, Z)
+            add(role, 0, mine, CORE)
+            wait_ready(1)
+            wait_ready(2)
+            send(role, 0, FAR_UP, FAR_DOWN)
+
+        @pl.when(step == 2)
+        def _():
+            add(role, 0, unit(0, y_up, 0), FAR_UP)
+            send(role, 0, UP)
+            add(role, 0, unit(0, y_down, 1), FAR_DOWN)
+            send(role, 0, DOWN)
+
+        @pl.when(step == 3)
+        def _():
+            add(role, 0, unit(0, y, 0), UP, DOWN)
+            send(role, 0, Z)
+            add(role, 1, unit(1, 0, z_lo), Z)
+            send(role, 1, FAR_UP, FAR_DOWN)
+
+        @pl.when(step == 4)
+        def _():
+            add(role, 1, unit(1, y_up, z_lo), FAR_UP)
+            send(role, 1, UP)
+            add(role, 1, unit(1, y_down, z_lo) + half, FAR_DOWN)
+            send(role, 1, DOWN)
+            add(role, 0, unit(0, y, z_lo), Z)
+            send_mirror(0)
+
+        @pl.when(step == 5)
+        def _():
+            add(role, 1, unit(1, y, z_lo), UP, DOWN)
+            send_mirror(1)
+
+        @pl.when(jnp.logical_and(step == 6, owner))
+        def _():
             for proj in range(2):
-                share_copy(role, proj, 0).wait_recv()
-                add(role, proj, mine, 0, 8 * SLICE)
-                if proj == 0:
-                    pl.semaphore_wait(ready_sem.at[role, 1], 1)
-                    pl.semaphore_wait(ready_sem.at[role, 2], 1)
-                share_copy(role, proj, 1).start()
-                share_copy(role, proj, 2).start()
-
-        @pl.when(step == 2)
-        def _():
-            for proj in range(2):
-                share_copy(role, proj, 1).wait_recv()
-                add(role, proj, unit(y_up, 0), 48, SLICE)
-                share_copy(role, proj, 3).start()
-                share_copy(role, proj, 2).wait_recv()
-                add(role, proj, unit(y_down, 1), 54, SLICE)
-                share_copy(role, proj, 4).start()
-
-        @pl.when(step == 3)
-        def _():
-            for proj in range(2):
-                share_copy(role, proj, 3).wait_recv()
-                share_copy(role, proj, 4).wait_recv()
-                add_two(role, proj, unit(y, 0), 60, 72, 2 * SLICE)
-                if proj == 0:
-                    pl.semaphore_wait(ready_sem.at[role, 3], 1)
-                share_copy(role, proj, 5).start()
-
-        @pl.when(step == 4)
-        def _():
-            for proj in range(2):
-                share_copy(role, proj, 5).wait_recv()
-                add(role, proj, unit(y, z_lo), 84, SLICE)
-
-                @pl.when(jnp.logical_not(owner))
-                def _(proj=proj):
-                    if proj == 0:
-                        pl.semaphore_wait(ready_sem.at[role, 4], 1)
-                    share_copy(role, proj, 6).start()
-
-        @pl.when(jnp.logical_and(step == 5, owner))
-        def _():
-            for proj in range(2):
-                share_copy(role, proj, 6).wait_recv()
-
-                def total(n, c, proj=proj):
+                share_copy(role, proj, MIRROR).wait_recv()
+                for n in range(SLICE):
                     there = WT[role, proj, 90 + n].astype(f32)
-                    sums_out[proj, n] = W[role, proj, unit(y, z_lo) + n].astype(f32) + there
-                    return c
-
-                lax.fori_loop(0, SLICE, total, 0)
+                    sums_out[proj, n] = W[role, proj, unit(proj, y, z_lo) + n].astype(f32) + there
 
     def turn(i, carry):
         code = jnp.int32(0)
@@ -609,12 +636,12 @@
     lax.fori_loop(0, 4 * chunks, drain, 0)
     for role in range(2):
         for proj in range(2):
-            for number in range(6):
+            for number in range(MIRROR):
                 share_copy(role, proj, number).wait_send()
 
             @pl.when(own != role)
             def _(role=role, proj=proj):
-                share_copy(role, proj, 6).wait_send()
+                share_copy(role, proj, MIRROR).wait_send()
 
 
 def adam_update(grad_sum, master, moment, variance, token_total):
@@ -628,17 +655,12 @@
 
 
 def shards(tokens, targets, weights, pattern, master, moment, variance):
-    section = lax.axis_index("section")
     dp_size = lax.axis_size("dp")
     row_count = tokens.shape[1] * tokens.shape[2]
     chunks = row_count // ROWS
 
-    def stream_rows(values):
-        mine = lax.dynamic_index_in_dim(values, section % 2, 0, keepdims=False)
-        return mine.reshape(row_count, DB, BS).transpose(1, 0, 2)
-
     index, keeps = tables(pattern[0])
-    orders = make_orders(chunks, 1.7, 2.3, 3.0)
+    orders = make_orders(chunks, 2.6, 2.5, 4.5)
     smem = pl.BlockSpec(memory_space=pltpu.SMEM)
     anywhere = pl.BlockSpec(memory_space=pl.ANY)
     grads = pl.pallas_call(
@@ -658,7 +680,7 @@
             pltpu.VMEM((DB, row_count, BS), bf16),
             pltpu.VMEM((NNZ + 1, ROWS, BS), f32),
             pltpu.SemaphoreType.DMA((2, 2)),
-            pltpu.SemaphoreType.DMA((2,)),
+            pltpu.SemaphoreType.DMA((2, DB)),
             pltpu.SemaphoreType.DMA((4, chunks)),
             pltpu.SemaphoreType.DMA((4, chunks)),
             pltpu.SemaphoreType.DMA((2, 2, 7)),
@@ -668,7 +690,7 @@
         compiler_params=pltpu.CompilerParams(
             collective_id=0, has_side_effects=True, vmem_limit_bytes=60 * 1024 * 1024
         ),
-    )(index, keeps, stream_rows(tokens), stream_rows(targets), weights[0])
+    )(index, keeps, tokens.reshape(2, row_count, D), targets.reshape(2, row_count, D), weights[0])
 
     token_total = 2 * row_count * dp_size
     step_direction, master_next = adam_update(

time: 221 us -> 211 us (0.955)
  Pallas kernels: 208 us -> 203 us
  local copies, waits for them, and re-layouts: 6.87 us -> 2.57 us
    pallas_call x1, Pallas kernels: 208 us -> 203 us  [shards(): pl.pallas_call(functools.partial(pipeline_kernel, chunks, make_sequences(...]
    reshape x2 -> x0, local copies, waits for them, and re-layouts: 2.38 us -> none  [stream_rows(): return mine.reshape(row_count, DB, BS).transpose(1, 0, 2)]
where the time goes in v3:
time: 211 us
  Pallas kernels  203 us (96%)
  other arithmetic  4.57 us (2%)
  local copies, waits for them, and re-layouts  2.57 us (1%)
    pallas_call x1, Pallas kernels, shards(): pl.pallas_call(functools.partial(pipeline_kernel, chunks, make_sequences(...  203 us

profile of v3, /device:TPU:0, one launch (start us, length us, event | category | flops | bytes accessed | tf_op | source)
XLA Modules:
  0.0 210.7 jit_solution(5458498459081620603)
XLA Ops:
  0.6 0.7 copy.41
  1.3 0.2 convert_reduce_fusion
  1.6 0.3 select_reduce_fusion
  1.9 0.1 compare_convert_fusion.2
  2.0 0.1 compare_convert_fusion.3
  2.1 0.1 compare_convert_fusion
  2.1 0.1 compare_convert_fusion.1
  2.2 0.1 concatenate.7
  2.3 0.6 reshape.70.keeps
  2.9 0.1 convert_reduce_fusion.3
  3.1 0.1 convert_reduce_fusion.7
  3.2 0.1 convert_reduce_fusion.5
  3.4 0.1 convert_reduce_fusion.1
  3.6 0.1 concatenate.6
  3.7 0.7 reshape.69.tab
  4.4 202.8 %shard_map.86 = f32[2,6,128,128]{3,2,1,0:T(8,128)} custom-call(s32[1856]{0:T(1024)} %reshape.69.tab, f32[768]{0:T(1024)} %reshape.70.keeps, bf16[2,224,2048]{2,1,0:T(8,128)(2,1)} %bitcast.47, bf16[2,224,2048]{2,1,0:T(8,128)(2,1)} %bitcast.48, bf16[2,2,96,128,128]{4,3,2,1,0:T(8,128)(2,1)} %bitcast.44), custom_call_target="tpu_custom_call" | custom-call | tf_op jit(solution)/shard_map/pallas_call | solution.py:666
  207.2 0.0 copy-start
  207.2 0.0 copy-start.1
  207.2 0.0 copy-start.2
  207.2 1.5 broadcast_multiply_fusion
  208.7 0.0 copy-done
  208.7 0.1 copy-done.1
  208.8 0.2 copy-done.2
  209.0 1.7 multiply_subtract_fusion
  (14 shorter events, 0.1 us)
Async XLA Ops:
  207.2 1.5 copy-start
  207.2 1.6 copy-start.1
  207.2 1.8 copy-start.2

commit v4 on v3

--- a/solution.py
+++ b/solution.py
@@ -67,7 +67,7 @@
     for order in orders:
         turn = order.index(2 * chunks + chunks - 1)
         code = lambda step, role: items + 2 * step + role
-        first = [(turn, 0)] + [(turn + gap, step) for step, gap in ((1, 2), (2, 4), (3, 7))]
+        first = [(turn, 0)] + [(turn + gap, step) for step, gap in ((1, 2), (2, 3), (3, 6))]
         placed = {}
         for at, step in first:
             if at < items - 1 and turn < items - 2:

time: 211 us -> 206 us (0.976)
  Pallas kernels: 203 us -> 197 us
    pallas_call x1, Pallas kernels: 203 us -> 197 us  [shards(): pl.pallas_call(functools.partial(pipeline_kernel, chunks, make_sequences(...]
where the time goes in v4:
time: 206 us; the launch traced here: 205 us
  Pallas kernels  197 us (96%)
  other arithmetic  4.57 us (2%)
  local copies, waits for them, and re-layouts  2.57 us (1%)
    pallas_call x1, Pallas kernels, shards(): pl.pallas_call(functools.partial(pipeline_kernel, chunks, make_sequences(...  197 us

profile of v4, /device:TPU:0, one launch (start us, length us, event | category | flops | bytes accessed | tf_op | source)
XLA Modules:
  0.0 204.9 jit_solution(14259252808010278975)
XLA Ops:
  0.6 0.7 copy.41
  1.3 0.2 convert_reduce_fusion
  1.6 0.3 select_reduce_fusion
  1.9 0.1 compare_convert_fusion.2
  2.0 0.1 compare_convert_fusion.3
  2.1 0.1 compare_convert_fusion
  2.1 0.1 compare_convert_fusion.1
  2.2 0.1 concatenate.7
  2.3 0.6 reshape.70.keeps
  2.9 0.1 convert_reduce_fusion.3
  3.1 0.1 convert_reduce_fusion.7
  3.2 0.1 convert_reduce_fusion.5
  3.4 0.1 convert_reduce_fusion.1
  3.6 0.1 concatenate.6
  3.7 0.7 reshape.69.tab
  4.4 197.0 %shard_map.86 = f32[2,6,128,128]{3,2,1,0:T(8,128)} custom-call(s32[1856]{0:T(1024)} %reshape.69.tab, f32[768]{0:T(1024)} %reshape.70.keeps, bf16[2,224,2048]{2,1,0:T(8,128)(2,1)} %bitcast.47, bf16[2,224,2048]{2,1,0:T(8,128)(2,1)} %bitcast.48, bf16[2,2,96,128,128]{4,3,2,1,0:T(8,128)(2,1)} %bitcast.44), custom_call_target="tpu_custom_call" | custom-call | tf_op jit(solution)/shard_map/pallas_call | solution.py:666
  201.4 0.0 copy-start
  201.4 0.0 copy-start.1
  201.4 0.0 copy-start.2
  201.4 1.5 broadcast_multiply_fusion
  202.9 0.0 copy-done
  202.9 0.1 copy-done.1
  203.0 0.2 copy-done.2
  203.2 1.7 multiply_subtract_fusion
  (14 shorter events, 0.1 us)
Async XLA Ops:
  201.4 1.5 copy-start
  201.4 1.6 copy-start.1
  201.4 1.8 copy-start.2

commit v5 on v4

--- a/solution.py
+++ b/solution.py
@@ -80,8 +80,9 @@
         early = [code(step, 1) for step in range(done, STEPS)]
         late = [code(step, 0) for step in range(STEPS)]
         if done == 0:
-            sequence.append(early.pop(0))
-        sequence.append(late.pop(0))
+            sequence.extend([early.pop(0), early.pop(0), late.pop(0)])
+        else:
+            sequence.extend([late.pop(0), late.pop(0)])
         while early or late:
             if early:
                 sequence.append(early.pop(0))

time: 206 us -> 207 us (level)
    pallas_call x1, Pallas kernels: 197 us -> 199 us  [shards(): pl.pallas_call(functools.partial(pipeline_kernel, chunks, make_sequences(...]
where the time goes in v5:
time: 207 us
  Pallas kernels  199 us (96%)
  other arithmetic  4.57 us (2%)
  local copies, waits for them, and re-layouts  2.57 us (1%)
    pallas_call x1, Pallas kernels, shards(): pl.pallas_call(functools.partial(pipeline_kernel, chunks, make_sequences(...  199 us

profile of v5, /device:TPU:0, one launch (start us, length us, event | category | flops | bytes accessed | tf_op | source)
XLA Modules:
  0.0 207.2 jit_solution(15081967104838256831)
XLA Ops:
  0.6 0.7 copy.41
  1.3 0.2 convert_reduce_fusion
  1.6 0.3 select_reduce_fusion
  1.9 0.1 compare_convert_fusion.2
  2.0 0.1 compare_convert_fusion.3
  2.1 0.1 compare_convert_fusion
  2.1 0.1 compare_convert_fusion.1
  2.2 0.1 concatenate.7
  2.3 0.6 reshape.70.keeps
  2.9 0.1 convert_reduce_fusion.3
  3.1 0.1 convert_reduce_fusion.7
  3.2 0.1 convert_reduce_fusion.5
  3.4 0.1 convert_reduce_fusion.1
  3.6 0.1 concatenate.6
  3.7 0.7 reshape.69.tab
  4.4 199.4 %shard_map.86 = f32[2,6,128,128]{3,2,1,0:T(8,128)} custom-call(s32[1856]{0:T(1024)} %reshape.69.tab, f32[768]{0:T(1024)} %reshape.70.keeps, bf16[2,224,2048]{2,1,0:T(8,128)(2,1)} %bitcast.47, bf16[2,224,2048]{2,1,0:T(8,128)(2,1)} %bitcast.48, bf16[2,2,96,128,128]{4,3,2,1,0:T(8,128)(2,1)} %bitcast.44), custom_call_target="tpu_custom_call" | custom-call | tf_op jit(solution)/shard_map/pallas_call | solution.py:667
  203.7 0.0 copy-start
  203.8 0.0 copy-start.1
  203.8 0.0 copy-start.2
  203.8 1.5 broadcast_multiply_fusion
  205.3 0.0 copy-done
  205.3 0.1 copy-done.1
  205.4 0.2 copy-done.2
  205.6 1.7 multiply_subtract_fusion
  (14 shorter events, 0.1 us)
Async XLA Ops:
  203.7 1.5 copy-start
  203.8 1.6 copy-start.1
  203.8 1.8 copy-start.2

commit v6 on v4

--- a/solution.py
+++ b/solution.py
@@ -474,7 +474,7 @@
     def unit(proj, of_y, of_z):
         return mine + (of_y * 2 + of_z if proj == 0 else of_z * 4 + of_y) * SLICE
 
-    CORE, FAR_UP, FAR_DOWN, UP, DOWN, Z, MIRROR = range(7)
+    CORE, FAR_UP, FAR_DOWN, UP, DOWN, Z, MIRROR, CORE_STAY = range(8)
     half = SLICE // 2
     copies = (
         (
@@ -487,13 +487,14 @@
             (unit(0, y, z_lo), 90, SLICE, mirror),
         ),
         (
-            ((1 - core) * 8 * SLICE, 0, 48, peer_core),
+            ((1 - core) * 8 * SLICE + (1 - z_lo) * 4 * SLICE, 0, 24, peer_core),
             (unit(1, y_far, z_lo), 48, half, peer_up),
             (unit(1, y_far, z_lo) + half, 51, half, peer_down),
             (unit(1, y_up, z_lo), 54, SLICE, peer_up),
             (unit(1, y_down, z_lo), 60, SLICE, peer_down),
             (unit(1, 0, 1 - z_lo), 66, 4 * SLICE, peer_z),
             (unit(1, y, z_lo), 90, SLICE, mirror),
+            ((1 - core) * 8 * SLICE + z_lo * 4 * SLICE, 24, 24, peer_core),
         ),
     )
 
@@ -553,16 +554,18 @@
             send(role, 1, CORE)
             weight_gradient(role, 0)
             send(role, 0, CORE)
+            send(role, 1, CORE_STAY)
 
         @pl.when(step == 1)
         def _():
-            add(role, 1, mine, CORE)
+            add(role, 1, unit(1, 0, 1 - z_lo), CORE)
             wait_ready(3)
             send(role, 1, Z)
             add(role, 0, mine, CORE)
             wait_ready(1)
             wait_ready(2)
             send(role, 0, FAR_UP, FAR_DOWN)
+            add(role, 1, unit(1, 0, z_lo), CORE_STAY)
 
         @pl.when(step == 2)
         def _():
@@ -638,6 +641,8 @@
         for proj in range(2):
             for number in range(MIRROR):
                 share_copy(role, proj, number).wait_send()
+            if proj == 1:
+                share_copy(role, proj, CORE_STAY).wait_send()
 
             @pl.when(own != role)
             def _(role=role, proj=proj):
@@ -683,8 +688,8 @@
             pltpu.SemaphoreType.DMA((2, DB)),
             pltpu.SemaphoreType.DMA((4, chunks)),
             pltpu.SemaphoreType.DMA((4, chunks)),
-            pltpu.SemaphoreType.DMA((2, 2, 7)),
-            pltpu.SemaphoreType.DMA((2, 2, 7)),
+            pltpu.SemaphoreType.DMA((2, 2, 8)),
+            pltpu.SemaphoreType.DMA((2, 2, 8)),
             pltpu.SemaphoreType.REGULAR((2, 5)),
         ],
         compiler_params=pltpu.CompilerParams(

time: 206 us -> 206 us (level)
  no operation moved by 1% of the time
where the time goes in v6:
time: 206 us; the launch traced here: 205 us
  Pallas kernels  197 us (96%)
  other arithmetic  4.57 us (2%)
  local copies, waits for them, and re-layouts  2.57 us (1%)
    pallas_call x1, Pallas kernels, shards(): pl.pallas_call(functools.partial(pipeline_kernel, chunks, make_sequences(...  197 us

profile of v6, /device:TPU:0, one launch (start us, length us, event | category | flops | bytes accessed | tf_op | source)
XLA Modules:
  0.0 205.1 jit_solution(5037062020269181081)
XLA Ops:
  0.6 0.7 copy.41
  1.3 0.2 convert_reduce_fusion
  1.6 0.3 select_reduce_fusion
  1.9 0.1 compare_convert_fusion.2
  2.0 0.1 compare_convert_fusion.3
  2.1 0.1 compare_convert_fusion
  2.1 0.1 compare_convert_fusion.1
  2.2 0.1 concatenate.7
  2.3 0.6 reshape.70.keeps
  2.9 0.1 convert_reduce_fusion.3
  3.1 0.1 convert_reduce_fusion.7
  3.2 0.1 convert_reduce_fusion.5
  3.4 0.1 convert_reduce_fusion.1
  3.6 0.1 concatenate.6
  3.7 0.7 reshape.69.tab
  4.4 197.2 %shard_map.86 = f32[2,6,128,128]{3,2,1,0:T(8,128)} custom-call(s32[1856]{0:T(1024)} %reshape.69.tab, f32[768]{0:T(1024)} %reshape.70.keeps, bf16[2,224,2048]{2,1,0:T(8,128)(2,1)} %bitcast.47, bf16[2,224,2048]{2,1,0:T(8,128)(2,1)} %bitcast.48, bf16[2,2,96,128,128]{4,3,2,1,0:T(8,128)(2,1)} %bitcast.44), custom_call_target="tpu_custom_call" | custom-call | tf_op jit(solution)/shard_map/pallas_call | solution.py:671
  201.6 0.0 copy-start
  201.6 0.0 copy-start.1
  201.6 0.0 copy-start.2
  201.6 1.5 broadcast_multiply_fusion
  203.1 0.0 copy-done
  203.1 0.1 copy-done.1
  203.2 0.2 copy-done.2
  203.5 1.7 multiply_subtract_fusion
  (14 shorter events, 0.1 us)
Async XLA Ops:
  201.6 1.5 copy-start
  201.6 1.6 copy-start.1
  201.6 1.8 copy-start.2
